TPU v7x, 128 devices: a whole 4x4x4 slice. The times are simulated.
128 devices in a mesh: seq: 8 (over y, core), tensor: 16 (over z, x).
Axes of the slice: x: 4, y: 4, z: 4, core: 2. Of those that a mesh axis runs over, the one named last changes fastest.
Arguments:
- hidden: bfloat16 [4096, 4096], P('seq', 'tensor'), may hold values from -40 to 40
- encoded: bfloat16 [64, 128, 4096], P('seq', None, 'tensor'), may hold values from -6 to 6
- w_query: bfloat16 [4096, 4096], P(None, 'tensor'), may hold values from -0.375 to 0.375
- w_key: bfloat16 [4096, 4096], P(None, 'tensor'), may hold values from -0.09375 to 0.09375
- w_value: bfloat16 [4096, 4096], P(None, 'tensor'), may hold values from -0.09375 to 0.09375
- w_out: bfloat16 [4096, 4096], P('tensor'), may hold values from -0.1875 to 0.1875
- send_rows: int32 [8, 16], P('seq'), may hold values from -1 to 7, as said below
- read_slot: int32 [64, 2], P('seq'), may hold values from 0 to 15, as said below
- grad_out: bfloat16 [4096, 4096], P('seq', 'tensor'), may hold values from -6 to 6
Outputs:
- out: bfloat16 [4096, 4096], P('seq', 'tensor')
- grad_hidden: bfloat16 [4096, 4096], P('seq', 'tensor')
- grad_encoded: bfloat16 [64, 128, 4096], P('seq', None, 'tensor')
Inputs may be any that keep to these rules, and one draw needn't show every extreme that they name: `send_rows`: for every owner and reading device the live slots come first, one to 2 of them, naming distinct local rows; padded slots hold -1. Some pairs have 2 live slots and some have one. `read_slot`: every entry names a live slot of the reading device; every live slot of a reading device is named by some span of that device.
All inputs are finite; a program needn't handle non-finite values.
Results may differ from a plain program's by a relative error of at most 0.029.
The roundings to bfloat16 on the way count: a program that leaves them out, or rounds other values in their place, can miss the bound.
Values may be sent and summed in bfloat16 or wider, within the bound.
A program may use at most 128 MiB of HBM per device.

v0:
```python
import jax
import jax.numpy as jnp
from jax import lax
from jax.sharding import PartitionSpec as P

SPAN = 64
NEIGH = 2
RLEN = 128
HEAD_DIM = 128


def passed_along(value, axis, steps):
    count = lax.axis_size(axis)
    first, last = (max(0, -steps), min(count, count - steps))
    return lax.ppermute(value, axis, [(source, source + steps) for source in range(first, last)])


def split_heads(block):
    return block.reshape(block.shape[0], block.shape[1], block.shape[2] // HEAD_DIM, HEAD_DIM)


def attend(block_q, block_k, block_v):
    scale = HEAD_DIM ** (-0.5)
    scores = (
        jnp.einsum(
            "bqhd,bkhd->bhqk",
            split_heads(block_q),
            split_heads(block_k),
            preferred_element_type=jnp.float32,
        )
        * scale
    )
    peak = jnp.max(scores, axis=-1, keepdims=True)
    weights = jnp.exp(scores - peak)
    probs = weights / jnp.sum(weights, axis=-1, keepdims=True)
    probs_low = probs.astype(jnp.bfloat16)
    context = jnp.einsum(
        "bhqk,bkhd->bqhd", probs_low, split_heads(block_v), preferred_element_type=jnp.float32
    )
    flat = context.astype(jnp.bfloat16).reshape(
        block_q.shape[0] * block_q.shape[1], block_q.shape[2]
    )
    return (probs, probs_low, flat)


def attend_grad(block_q, block_k, block_v, probs, probs_low, grad_block):
    scale = HEAD_DIM ** (-0.5)
    batch, width = (block_q.shape[0], block_q.shape[2])
    grad_heads = split_heads(grad_block)
    grad_probs = jnp.einsum(
        "bqhd,bkhd->bhqk", grad_heads, split_heads(block_v), preferred_element_type=jnp.float32
    )
    grad_values = jnp.einsum(
        "bhqk,bqhd->bkhd", probs_low, grad_heads, preferred_element_type=jnp.float32
    )
    grad_scores = probs * (grad_probs - jnp.sum(grad_probs * probs, axis=-1, keepdims=True))
    scaled = (grad_scores * scale).astype(jnp.bfloat16)
    grad_queries = jnp.einsum(
        "bhqk,bkhd->bqhd", scaled, split_heads(block_k), preferred_element_type=jnp.float32
    )
    grad_keys = jnp.einsum(
        "bhqk,bqhd->bkhd", scaled, split_heads(block_q), preferred_element_type=jnp.float32
    )
    grad_queries = grad_queries.astype(jnp.bfloat16).reshape(batch * block_q.shape[1], width)
    return (
        grad_queries,
        grad_keys.reshape(batch, -1, width),
        grad_values.reshape(batch, -1, width),
    )


def per_device(hidden, encoded, w_query, w_key, w_value, w_out, send_rows, read_slot, grad_out):
    token_rows = hidden.shape[0]
    local_width = w_query.shape[1]
    offset_rows = SPAN - 1
    spans_here = token_rows // SPAN
    owned = encoded.shape[0]
    owned_rows = owned * RLEN
    slots_all = send_rows.shape[1]
    queries = jnp.dot(
        lax.all_gather(hidden, "tensor", axis=1, tiled=True),
        w_query,
        preferred_element_type=jnp.float32,
    ).astype(jnp.bfloat16)
    piece = lax.all_gather(encoded, "tensor", axis=2, tiled=True)
    columns = piece.shape[2]
    flat = piece.reshape(owned_rows, columns)
    key_sums = jnp.dot(flat, w_key, preferred_element_type=jnp.float32)
    value_sums = jnp.dot(flat, w_value, preferred_element_type=jnp.float32)
    keys = key_sums.astype(jnp.bfloat16).reshape(owned, RLEN, local_width)
    values = value_sums.astype(jnp.bfloat16).reshape(owned, RLEN, local_width)
    targets = send_rows[0]
    safe_rows = jnp.maximum(targets, 0)
    outgoing = jnp.stack([keys[safe_rows], values[safe_rows]], 1)
    incoming = lax.all_to_all(outgoing, "seq", split_axis=0, concat_axis=0, tiled=True)
    slot_ids = read_slot.reshape(-1)
    span_pairs = incoming[slot_ids].reshape(spans_here, NEIGH, 2, RLEN, local_width)
    span_pairs = span_pairs.transpose(0, 2, 1, 3, 4).reshape(
        spans_here, 2, NEIGH * RLEN, local_width
    )
    edge_pairs = passed_along(span_pairs[spans_here - 1], "seq", 1)
    block_pairs = jnp.concatenate([edge_pairs[None], span_pairs], 0)
    lead = jnp.zeros((1, local_width), jnp.bfloat16)
    trail = jnp.zeros((offset_rows, local_width), jnp.bfloat16)
    block_q = jnp.concatenate([lead, queries, trail], 0).reshape(spans_here + 1, SPAN, local_width)
    probs, probs_low, context = attend(block_q, block_pairs[:, 0], block_pairs[:, 1])
    attended = context[1 : 1 + token_rows]
    partial_out = jnp.dot(attended, w_out, preferred_element_type=jnp.float32)
    out = lax.psum_scatter(
        partial_out.astype(jnp.bfloat16), "tensor", scatter_dimension=1, tiled=True
    )
    grad_attended = lax.dot_general(
        lax.all_gather(grad_out, "tensor", axis=1, tiled=True),
        w_out,
        (((1,), (1,)), ((), ())),
        preferred_element_type=jnp.float32,
    ).astype(jnp.bfloat16)
    lead = jnp.zeros((1, local_width), jnp.bfloat16)
    trail = jnp.zeros((offset_rows, local_width), jnp.bfloat16)
    grad_block = jnp.concatenate([lead, grad_attended, trail], 0).reshape(
        spans_here + 1, SPAN, local_width
    )
    grad_q, grad_k, grad_v = attend_grad(
        block_q, block_pairs[:, 0], block_pairs[:, 1], probs, probs_low, grad_block
    )
    grad_queries = grad_q[1 : 1 + token_rows]
    edge_grads = passed_along(jnp.stack([grad_k[0], grad_v[0]], 0), "seq", -1)
    read_keys = grad_k[1:].at[spans_here - 1].add(edge_grads[0])
    read_values = grad_v[1:].at[spans_here - 1].add(edge_grads[1])
    slot_hot = (slot_ids[None, :] == jnp.arange(slots_all, dtype=jnp.int32)[:, None]).astype(
        jnp.float32
    )
    read_flat = RLEN * local_width
    slot_keys = jnp.dot(
        slot_hot, read_keys.reshape(spans_here * NEIGH, read_flat), precision=lax.Precision.HIGHEST
    )
    slot_values = jnp.dot(
        slot_hot,
        read_values.reshape(spans_here * NEIGH, read_flat),
        precision=lax.Precision.HIGHEST,
    )
    slot_grads = (
        jnp.stack([slot_keys, slot_values], 1)
        .astype(jnp.bfloat16)
        .reshape(slots_all, 2, RLEN, local_width)
    )
    owner_grads = lax.all_to_all(slot_grads, "seq", split_axis=0, concat_axis=0, tiled=True)
    owner_hot = (targets[None, :] == jnp.arange(owned, dtype=jnp.int32)[:, None]).astype(
        jnp.bfloat16
    )
    owner_sums = jnp.dot(
        owner_hot, owner_grads.reshape(slots_all, 2 * read_flat), preferred_element_type=jnp.float32
    )
    owner_sums = owner_sums.astype(jnp.bfloat16).reshape(owned, 2, RLEN, local_width)
    grad_key_rows = owner_sums[:, 0].reshape(owned_rows, local_width)
    grad_value_rows = owner_sums[:, 1].reshape(owned_rows, local_width)
    contract = (((1,), (1,)), ((), ()))
    partial_enc = lax.dot_general(
        grad_key_rows, w_key, contract, preferred_element_type=jnp.float32
    )
    partial_enc = partial_enc + lax.dot_general(
        grad_value_rows, w_value, contract, preferred_element_type=jnp.float32
    )
    partial_enc = partial_enc.reshape(owned, RLEN, partial_enc.shape[1])
    grad_encoded = lax.psum_scatter(
        partial_enc.astype(jnp.bfloat16), "tensor", scatter_dimension=2, tiled=True
    )
    partial_hidden = lax.dot_general(
        grad_queries, w_query, contract, preferred_element_type=jnp.float32
    )
    grad_hidden = lax.psum_scatter(
        partial_hidden.astype(jnp.bfloat16), "tensor", scatter_dimension=1, tiled=True
    )
    return (out, grad_hidden, grad_encoded)


def solution(mesh):
    placed = (
        P("seq", "tensor"),
        P("seq", None, "tensor"),
        P(None, "tensor"),
        P(None, "tensor"),
        P(None, "tensor"),
        P("tensor", None),
        P("seq", None),
        P("seq", None),
        P("seq", "tensor"),
    )
    return jax.shard_map(
        per_device,
        mesh=mesh,
        in_specs=placed,
        out_specs=(P("seq", "tensor"), P("seq", "tensor"), P("seq", None, "tensor")),
        check_vma=False,
    )
```

profile of v0, /device:TPU:0, one launch (start us, length us, event | category | flops | bytes accessed | tf_op | source)
XLA Modules:
  0.0 488.8 jit_solution(10911002069055826108)
XLA Ops:
  7.2 0.7 all-gather.4.cloned.1.call-update
  8.0 0.7 all-gather.6.cloned.1.call-update
  8.7 0.7 all-gather.8.cloned.1.call-update
  9.4 0.7 maximum_bitcast_fusion
  10.1 81.0 %all-gather.4.cloned.1.call-done = bf16[8,128,4096]{2,1,0:T(8,128)(2,1)} async-done(((bf16[8,128,256]{2,1,0:T(8,128)(2,1)}), bf16[8,128,4096]{2,1,0:T(8,128)(2,1)}) %all-gather.4.cloned.1.call-update) | async-done | bytes 8388624 | tf_op jit(solution)/shard_map/all_gather | solution.py:85
  91.1 7.1 %convolution_convert_fusion.3 = bf16[1024,256]{1,0:T(8,128)(2,1)} fusion(bf16[1024,4096]{1,0:T(8,128)(2,1)} %bitcast.130, bf16[4096,256]{1,0:T(8,128)(2,1)} %param.17), kind=kOutput, calls=%fused_computation.32 | convolution fusion | flops 2147745792 | bytes 11010048 | tf_op jit(solution)/shard_map/dot_general | solution.py:89
  98.2 1.7 gather_fusion.1
  99.9 6.7 %convolution_convert_fusion.4 = bf16[1024,256]{1,0:T(8,128)(2,1)} fusion(bf16[1024,4096]{1,0:T(8,128)(2,1)} %bitcast.131, bf16[4096,256]{1,0:T(8,128)(2,1)S(1)} %copy-done), kind=kOutput, calls=%fused_computation.33 | convolution fusion | flops 2147745792 | bytes 11010048 | tf_op jit(solution)/shard_map/dot_general | solution.py:88
  106.6 2.6 gather_fusion
  109.2 2.7 pad_maximum_fusion
  111.9 4.5 all-to-all-start
  116.7 33.5 %all-gather.6.cloned.1.call-done = bf16[512,4096]{1,0:T(8,128)(2,1)} async-done(((bf16[512,256]{1,0:T(8,128)(2,1)}), bf16[512,4096]{1,0:T(8,128)(2,1)}) %all-gather.6.cloned.1.call-update) | async-done | bytes 4194320 | tf_op jit(solution)/shard_map/all_gather | solution.py:81
  150.2 4.1 convolution_convert_fusion.8
  154.3 3.6 gather_fusion.2
  157.9 1.0 slice.127
  158.9 1.5 collective-permute-start
  160.4 48.9 %all-gather.8.cloned.1.call-done = bf16[512,4096]{1,0:T(8,128)(2,1)} async-done(((bf16[512,256]{1,0:T(8,128)(2,1)}), bf16[512,4096]{1,0:T(8,128)(2,1)}) %all-gather.8.cloned.1.call-update) | async-done | bytes 4194320 | tf_op jit(solution)/shard_map/all_gather | solution.py:113
  209.3 4.1 convolution_convert_fusion.7
  213.5 1.0 maximum_maximum_fusion.1
  214.5 0.8 reshape_reshape.7
  215.3 1.7 copy.72
  217.0 1.2 pad_maximum_fusion.2
  218.3 2.4 copy.74
  220.7 1.5 copy.73
  222.2 1.7 convolution_multiply_fusion
  223.9 1.3 fusion.61
  225.2 4.1 fusion.27
  229.3 1.3 copy.78
  230.6 4.8 convolution_convert_fusion.2
  235.5 1.7 reshape_reshape.8
  237.2 2.7 fusion.43
  239.9 9.5 %fusion.28 = bf16[9,64,2,128]{3,1,2,0:T(8,128)(2,1)} fusion(bf16[9,256,2,128]{1,3,2,0:T(8,128)(2,1)} %bitcast.109, f32[9,2,64,256]{3,2,1,0:T(8,128)} %fusion.43, f32[9,2,64,256]{3,2,1,0:T(8,128)} %get-tuple-element.40, f32[9,2,64]{2,1,0:T(2,128)S(1)} %get-tuple-element.39), kind=kOutput, calls=%fused_computation.41 | convolution fusion | flops 77710720 | bytes 3838464 | tf_op jit(solution)/shard_map/bhqk,bkhd->bqhd/dot_general | solution.py:58
  249.5 1.3 copy.82
  250.8 4.8 convolution_convert_fusion.1
  255.7 0.3 reduce-scatter.8.cloned.1.call-start
  255.9 10.5 %convolution_bitcast_fusion.1 = f32[9,256,2,128]{1,3,2,0:T(8,128)} fusion(f32[9,2,64,256]{3,2,1,0:T(8,128)} %fusion.43, bf16[9,64,2,128]{3,2,1,0:T(2,128)(2,1)} %reshape_reshape.7, f32[9,2,64,256]{3,2,1,0:T(8,128)} %get-tuple-element.40, f32[9,2,64]{2,1,0:T(2,128)S(1)} %get-tuple-element.39), kind=kOutput, calls=%fused_computation.20 | convolution fusion | flops 77563264 | bytes 5018112 | tf_op jit(solution)/shard_map/bhqk,bqhd->bkhd/dot_general | solution.py:61
  266.4 1.8 fusion.58
  268.2 1.8 copy.86
  270.0 4.7 convolution_bitcast_fusion
  274.7 1.1 fusion.59
  275.8 0.1 copy.87
  275.9 1.8 pad_maximum_fusion.3
  277.7 1.3 collective-permute-start.1
  279.1 3.4 slice.132
  282.4 1.5 slice.137
  284.0 2.9 copy.89
  286.9 0.1 copy.88
  287.1 2.9 copy.92
  290.0 0.1 copy.91
  290.1 1.9 fusion.39
  292.0 2.8 reshape.187
  294.8 2.8 reshape.190
  297.5 3.0 fusion.22
  300.5 1.1 fusion.19
  301.6 0.2 pad_maximum_fusion.1
  301.8 0.7 copy.94
  302.5 32.7 %all_to_all.10 = bf16[16,2,128,256]{3,2,1,0:T(8,128)(2,1)S(1)} all-to-all(bf16[16,2,128,256]{3,2,1,0:T(8,128)(2,1)S(1)} %copy.94), channel_id=1, replica_groups=mesh['seq'=8,'tensor'=16] {'seq'}, dimensions={0} | all-to-all | bytes 4194304 | tf_op jit(solution)/shard_map/all_to_all | solution.py:147
  335.3 1.2 copy.107
  336.5 0.4 convolution_convert_fusion
  337.0 0.1 copy.102
  337.2 8.1 %fusion.62 = f32[1024,4096]{1,0:T(8,128)} fusion(bf16[1024,256]{1,0:T(8,128)(2,1)S(1)} %bitcast.117, bf16[4096,256]{1,0:T(8,128)(2,1)S(1)} %copy-done), kind=kOutput, calls=%fused_computation.84 | convolution fusion | flops 2147483648 | bytes 19398656 | tf_op jit(solution)/shard_map/dot_general | solution.py:158
  345.3 11.8 %add_convert_fusion = bf16[1024,4096]{1,0:T(8,128)(2,1)} fusion(f32[1024,4096]{1,0:T(8,128)} %fusion.62, bf16[1024,256]{1,0:T(8,128)(2,1)S(1)} %bitcast.115, bf16[4096,256]{1,0:T(8,128)(2,1)S(1)} %copy-done.3), kind=kOutput, calls=%fused_computation.6 | convolution fusion | flops 2155872256 | bytes 27787264 | tf_op jit(solution)/shard_map/dot_general | solution.py:161
  357.2 36.6 %reduce-scatter.6.cloned.1.call-done = bf16[512,256]{1,0:T(8,128)(2,1)} async-done(((bf16[512,4096]{1,0:T(8,128)(2,1)}), bf16[512,256]{1,0:T(8,128)(2,1)}) %reduce-scatter.6.cloned.1.call-update) | async-done | bytes 262160 | tf_op jit(solution)/shard_map/reduce_scatter | solution.py:171
  393.8 88.2 %reduce-scatter.8.cloned.1.call-done = bf16[8,128,256]{2,1,0:T(8,128)(2,1)} async-done(((bf16[8,128,4096]{2,1,0:T(8,128)(2,1)}), bf16[8,128,256]{2,1,0:T(8,128)(2,1)}) %reduce-scatter.8.cloned.1.call-update) | async-done | bytes 524304 | tf_op jit(solution)/shard_map/reduce_scatter | solution.py:165
  (38 shorter events, 0.9 us)
Async XLA Ops:
  7.2 92.7 %copy-start = (bf16[4096,256]{1,0:T(8,128)(2,1)S(1)}, bf16[4096,256]{1,0:T(8,128)(2,1)}, u32[]{:S(2)}) copy-start(bf16[4096,256]{1,0:T(8,128)(2,1)} %param.16) | copy-start | bytes 6291460
  7.2 83.9 %all-gather.4.cloned.1.call-start = ((), (), s32[]{:S(2)}) async-start(), calls=%async_computation.5 | async-start | bytes 8912896 | tf_op jit(solution)/shard_map/all_gather | solution.py:85
  7.9 142.3 %all-gather.6.cloned.1.call-start = ((), (), s32[]{:S(2)}) async-start(), calls=%async_computation.6 | async-start | bytes 4456448 | tf_op jit(solution)/shard_map/all_gather | solution.py:81
  8.7 200.7 %all-gather.8.cloned.1.call-start = ((), (), s32[]{:S(2)}) async-start(), calls=%async_computation.8 | async-start | bytes 4456448 | tf_op jit(solution)/shard_map/all_gather | solution.py:113
  111.9 4.6 copy-start.4
  111.9 42.4 %all-to-all-start = ((bf16[16,2,128,256]{3,2,1,0:T(8,128)(2,1)}), bf16[16,2,128,256]{3,2,1,0:T(8,128)(2,1)}, u32[]{:S(2)}, u32[]{:S(2)}) async-start(bf16[16,2,128,256]{3,2,1,0:T(8,128)(2,1)} %pad_maximum_fusion), calls=%async_computation | async-start | bytes 4194304 | tf_op jit(solution)/shard_map/all_to_all | solution.py:95
  116.4 240.8 %reduce-scatter.4.cloned.1.call-start = ((), (), s32[]{:S(2)}) async-start(), calls=%async_computation.7 | async-start | bytes 4456448 | tf_op jit(solution)/shard_map/reduce_scatter | solution.py:109
  158.9 58.1 %collective-permute-start = (bf16[2,256,256]{2,1,0:T(8,128)(2,1)S(1)}, bf16[2,256,256]{2,1,0:T(8,128)(2,1)S(1)}, u32[]{:S(2)}, u32[]{:S(2)}) collective-permute-start(bf16[2,256,256]{2,1,0:T(8,128)(2,1)S(1)} %bitcast.128), channel_id=1, source_target_pairs={{0,16},{16,32},{32,48},{48,64},{64,80},{80,96},{96,112},{1,17},{17... | collective-permute-start | bytes 786440 | tf_op jit(solution)/shard_map/ppermute | solution.py:15
  235.4 158.3 %reduce-scatter.6.cloned.1.call-start = ((), (), s32[]{:S(2)}) async-start(), calls=%async_computation.9 | async-start | bytes 4456448 | tf_op jit(solution)/shard_map/reduce_scatter | solution.py:171
  255.7 226.3 %reduce-scatter.8.cloned.1.call-start = ((), (), s32[]{:S(2)}) async-start(), calls=%async_computation.10 | async-start | bytes 8912896 | tf_op jit(solution)/shard_map/reduce_scatter | solution.py:165
  277.7 12.4 %collective-permute-start.1 = (f32[2,256,256]{2,1,0:T(8,128)}, f32[2,256,256]{2,1,0:T(8,128)}, u32[]{:S(2)}, u32[]{:S(2)}) collective-permute-start(f32[2,256,256]{2,1,0:T(8,128)} %pad_maximum_fusion.3), channel_id=1, source_target_pairs={{16,0},{32,16},{48,32},{64,48},{80,64},{96,80},{112,96},{17,1},{33... | collective-permute-start | bytes 1572872 | tf_op jit(solution)/shard_map/ppermute | solution.py:15
  279.1 3.4 copy-start.2
  297.5 3.0 copy-start.1
  335.3 1.2 copy-start.5
  337.2 8.1 %copy-start.3 = (bf16[4096,256]{1,0:T(8,128)(2,1)S(1)}, bf16[4096,256]{1,0:T(8,128)(2,1)}, u32[]{:S(2)}) copy-start(bf16[4096,256]{1,0:T(8,128)(2,1)} %param.17) | copy-start | bytes 6291460
Sparse Core Ops, SparseCore 0:
  10.1 80.9 all-gather.3
  93.2 56.9 all-gather.5
  152.3 56.9 all-gather.7
  235.5 77.0 reduce-scatter.3
  316.8 76.9 reduce-scatter.5
  397.6 84.3 reduce-scatter.7
where the time goes:
time: 490 us; the launch traced here: 489 us
  waiting for transfers between devices  290 us (59%)
  matrix products  89.3 us (18%)
  local copies, waits for them, and re-layouts  43.6 us (9%)
  blocking collectives  32.7 us (7%)
  between operations  14.4 us (3%)
  other arithmetic  10.8 us (2%)
  starting transfers between devices  7.7 us (2%)
    reduce_scatter x1, waiting for transfers between devices, per_device(): lax.psum_scatter(partial_enc.astype(jnp.bfloat16), 'tensor', scatter_dime...  88.2 us
    all_gather x1, waiting for transfers between devices, per_device(): piece = lax.all_gather(encoded, 'tensor', axis=2, tiled=True)  81 us
    all_gather x1, waiting for transfers between devices, per_device(): lax.all_gather(grad_out, 'tensor', axis=1, tiled=True)  48.9 us
    reduce_scatter x1, waiting for transfers between devices, per_device(): lax.psum_scatter(partial_hidden.astype(jnp.bfloat16), 'tensor', scatter_d...  36.6 us
    all_gather x1, waiting for transfers between devices, per_device(): lax.all_gather(hidden, 'tensor', axis=1, tiled=True)  33.5 us
    all_to_all x1, blocking collectives, per_device(): lax.all_to_all(slot_grads, 'seq', split_axis=0, concat_axis=0, tiled=True)  32.7 us
    dot_general x1, matrix products, per_device(): lax.dot_general(grad_value_rows, w_value, contract, preferred_element_typ...  11.8 us
    dot_general x1, matrix products, attend_grad(): jnp.einsum('bhqk,bqhd->bkhd', scaled, split_heads(block_q), preferred_ele...  10.5 us
  transfers between devices with their start and end apart: 9, of which 5 were waited for; matrix products, arithmetic and copies ran while one was open for 26% of the time, Pallas kernels for 0%

commit v1 on v0

v1 whole, which is shorter than its diff:
```python
import functools

import jax
import jax.numpy as jnp
from jax import lax
from jax.experimental import pallas as pl
from jax.experimental.pallas import tpu as pltpu
from jax.sharding import PartitionSpec as P

SPAN = 64
NEIGH = 2
RLEN = 128
HEAD_DIM = 128
NSEQ = 8
SIDE = 4
NT = SIDE * SIDE
W = 256
ROWS = 512
MESH = pl.DeviceIdType.MESH
ANY = pl.BlockSpec(memory_space=pl.ANY)
VM = pl.BlockSpec(memory_space=pltpu.VMEM)
SM = pl.BlockSpec(memory_space=pltpu.SMEM)
F32 = jnp.float32
BF16 = jnp.bfloat16
NT_DIMS = (((1,), (1,)), ((), ()))
TN_DIMS = (((0,), (0,)), ((), ()))


def wrap(value, count):
    return lax.rem(value + count, count)


class Grid:
    def __init__(self):
        self.seq = lax.axis_index("seq")
        tensor = lax.axis_index("tensor")
        self.z = lax.div(tensor, SIDE)
        self.x = lax.rem(tensor, SIDE)

    def first(self, order):
        return self.z if order == "zx" else self.x

    def second(self, order):
        return self.x if order == "zx" else self.z

    def block(self, order, b, a):
        return a * SIDE + b if order == "zx" else b * SIDE + a

    def along_first(self, order, step):
        a = wrap(self.first(order) + step, SIDE)
        return {"tensor": self.block(order, self.second(order), a)}

    def along_second(self, order, step):
        b = wrap(self.second(order) + step, SIDE)
        return {"tensor": self.block(order, b, self.first(order))}

    def along_seq(self, step):
        return {"seq": wrap(self.seq + step, NSEQ)}

    def barrier(self):
        sem = pltpu.get_barrier_semaphore()
        peers = [self.along_first("zx", 1), self.along_first("zx", -1)]
        peers += [self.along_second("zx", 1), self.along_second("zx", -1)]
        peers += [self.along_seq(k) for k in range(1, NSEQ)]
        for peer in peers:
            pl.semaphore_signal(sem, inc=1, device_id=peer, device_id_type=MESH)
        pl.semaphore_wait(sem, len(peers))


class Messages:
    def __init__(self, send, recv):
        self.send, self.recv, self.sent = send, recv, []

    def start(self, m, src, dst, peer):
        copy = pltpu.make_async_remote_copy(
            src_ref=src,
            dst_ref=dst,
            send_sem=self.send.at[m],
            recv_sem=self.recv.at[m],
            device_id=peer,
            device_id_type=MESH,
        )
        copy.start()
        self.sent.append(copy)

    def wait(self, m, dst):
        pltpu.make_async_copy(dst, dst, self.recv.at[m]).wait()

    def finish(self):
        for copy in self.sent:
            copy.wait_send()
        self.sent = []


class Gather:
    def __init__(self, grid, order, own, buf, send, recv):
        self.g, self.order, self.own, self.buf = grid, order, own, buf
        self.msg = Messages(send, recv)
        self.a, self.b = grid.first(order), grid.second(order)

    def slot(self, db, da):
        return self.buf.at[wrap(self.b + db, SIDE), wrap(self.a + da, SIDE)]

    def second(self, da, src=None):
        src = self.slot(0, da) if src is None else src
        for i, step in enumerate((1, -1)):
            peer = self.g.along_second(self.order, step)
            self.msg.start(4 + 2 * da + i, src, self.slot(0, da), peer)

    def start_first(self):
        for i, step in enumerate((1, -1)):
            peer = self.g.along_first(self.order, step)
            self.msg.start(i, self.own, self.slot(0, 0), peer)

    def start_second(self):
        self.second(0, self.own)

    def stage1(self):
        half = ROWS // 2
        low, high = pl.ds(0, half), pl.ds(half, half)
        self.msg.wait(0, self.slot(0, 3))
        part = self.slot(0, 3).at[low]
        self.msg.start(2, part, part, self.g.along_first(self.order, 1))
        self.second(3)
        self.msg.wait(1, self.slot(0, 1))
        part = self.slot(0, 1).at[high]
        self.msg.start(3, part, part, self.g.along_first(self.order, -1))
        self.second(1)

    def stage2(self):
        self.msg.wait(4, self.slot(3, 0))
        self.msg.start(12, self.slot(3, 0), self.slot(3, 0), self.g.along_second(self.order, 1))
        self.msg.wait(5, self.slot(1, 0))

    def stage3(self):
        half = ROWS // 2
        self.msg.wait(2, self.slot(0, 2).at[pl.ds(0, half)])
        self.msg.wait(3, self.slot(0, 2).at[pl.ds(half, half)])
        self.second(2)

    def stage4(self):
        self.msg.wait(4 + 6, self.slot(3, 3))
        self.msg.wait(5 + 6, self.slot(1, 3))
        self.msg.start(14, self.slot(1, 3), self.slot(1, 3), self.g.along_second(self.order, -1))
        self.msg.wait(4 + 2, self.slot(3, 1))
        self.msg.start(13, self.slot(3, 1), self.slot(3, 1), self.g.along_second(self.order, 1))
        self.msg.wait(5 + 2, self.slot(1, 1))

    def stage5(self):
        self.msg.wait(4 + 4, self.slot(3, 2))
        self.msg.wait(5 + 4, self.slot(1, 2))
        self.msg.start(15, self.slot(1, 2), self.slot(1, 2), self.g.along_second(self.order, -1))

    def stage6(self):
        for m, da in ((12, 0), (13, 1), (14, 3), (15, 2)):
            self.msg.wait(m, self.slot(2, da))

    def consume(self, db, use):
        b = wrap(self.b + db, SIDE)

        @pl.loop(0, SIDE)
        def _(a):
            use(self.buf.at[b, a], self.g.block(self.order, b, a))


def gather_kernel(
    enc_ref, hid_ref, gout_ref, wq_ref, wk_ref, wv_ref, wo_ref, rows_ref,
    q_ref, ga_ref, kv_ref,
    enc_lo, enc_hi, hid_all, gout_all, wq, wk, wv, wo, acc_k, acc_v, own_kv, stage, q_low, ga_low,
    send, recv, seq_send, seq_recv, edge_send, edge_recv, local,
):
    g = Grid()
    local_copies = [
        pltpu.make_async_copy(src, dst, local.at[i])
        for i, (src, dst) in enumerate(
            ((wk_ref, wk), (wv_ref, wv), (wq_ref, wq), (wo_ref, wo))
        )
    ]
    lo, hi = enc_ref.at[pl.ds(0, ROWS)], enc_ref.at[pl.ds(ROWS, ROWS)]
    streams = []
    for i, (order, own, buf) in enumerate(
        (("zx", lo, enc_lo), ("xz", hi, enc_hi), ("zx", hid_ref, hid_all), ("xz", gout_ref, gout_all))
    ):
        stream = Gather(g, order, own, buf, send.at[i], recv.at[i])
        streams.append(stream)
        local_copies.append(pltpu.make_async_copy(own, stream.slot(0, 0), local.at[4 + i]))
    enc, act = streams[:2], streams[2:]
    g.barrier()
    for s in enc:
        s.start_first()
    for s in enc:
        s.start_second()
    for copy in local_copies:
        copy.start()
    acc_k[...] = jnp.zeros_like(acc_k)
    acc_v[...] = jnp.zeros_like(acc_v)
    for s in enc:
        s.stage1()
    for s in enc:
        s.stage2()
    for s in enc:
        s.stage3()
    for s in act:
        s.start_first()
    for s in act:
        s.start_second()
    for copy in local_copies:
        copy.wait()

    def keys_values(i):
        def use(block, t):
            depth = pl.ds(pl.multiple_of(t * W, W), W)
            acc_k[i] += jnp.dot(block[...], wk[depth, :], preferred_element_type=F32)
            acc_v[i] += jnp.dot(block[...], wv[depth, :], preferred_element_type=F32)

        return use

    for i, s in enumerate(enc):
        s.consume(0, keys_values(i))
    for s in enc:
        s.stage4()
    for s in enc:
        s.stage5()
    for i, s in enumerate(enc):
        s.consume(3, keys_values(i))
        s.consume(1, keys_values(i))
    for s in act:
        s.stage1()
    for s in enc:
        s.stage6()
    for i, s in enumerate(enc):
        s.consume(2, keys_values(i))
    per_half = ROWS // RLEN
    for n in range(2 * per_half):
        rows = pl.ds((n % per_half) * RLEN, RLEN)
        own_kv[n, 0] = acc_k[n // per_half, rows, :].astype(BF16)
        own_kv[n, 1] = acc_v[n // per_half, rows, :].astype(BF16)

    @pl.loop(0, NSEQ)
    def _(r):
        for s in range(2):
            stage[r, s] = own_kv[jnp.maximum(rows_ref[0, 2 * r + s], 0)]

    seq_msg = Messages(seq_send, seq_recv)
    for k in range(1, NSEQ):
        peer = wrap(g.seq + k, NSEQ)
        seq_msg.start(k, stage.at[peer], kv_ref.at[g.seq], {"seq": peer})
    keep = pltpu.make_async_copy(stage.at[g.seq], kv_ref.at[g.seq], local.at[8])
    keep.start()

    acc_k[...] = jnp.zeros_like(acc_k)
    for s in act:
        s.stage2()
    for s in act:
        s.stage3()

    def queries(block, t):
        depth = pl.ds(pl.multiple_of(t * W, W), W)
        acc_k[0] += jnp.dot(block[...], wq[depth, :], preferred_element_type=F32)

    def grads(block, t):
        depth = pl.ds(pl.multiple_of(t * W, W), W)
        acc_k[1] += lax.dot_general(
            block[...], wo[:, depth], NT_DIMS, preferred_element_type=F32
        )

    uses = (queries, grads)
    for i, s in enumerate(act):
        s.consume(0, uses[i])
    for s in act:
        s.stage4()
    for s in act:
        s.stage5()
    for i, s in enumerate(act):
        s.consume(3, uses[i])
        s.consume(1, uses[i])
    for s in act:
        s.stage6()
    for i, s in enumerate(act):
        s.consume(2, uses[i])
    q_low[...] = acc_k[0].astype(BF16)
    ga_low[...] = acc_k[1].astype(BF16)
    edge = Messages(edge_send, edge_recv)
    head, tail, body = pl.ds(0, SPAN), pl.ds(ROWS, SPAN), pl.ds(0, ROWS)
    edge.start(0, q_low.at[head], q_ref.at[tail], g.along_seq(-1))
    edge.start(1, ga_low.at[head], ga_ref.at[tail], g.along_seq(-1))
    out_copies = [
        pltpu.make_async_copy(q_low, q_ref.at[body], local.at[0]),
        pltpu.make_async_copy(ga_low, ga_ref.at[body], local.at[1]),
    ]
    for copy in out_copies:
        copy.start()
    for s in streams:
        s.msg.finish()
    seq_msg.finish()
    edge.finish()
    for copy in out_copies:
        copy.wait()
    keep.wait()
    for k in range(1, NSEQ):
        seq_msg.wait(k, kv_ref.at[wrap(g.seq - k, NSEQ)])
    edge.wait(0, q_ref.at[tail])
    edge.wait(1, ga_ref.at[tail])


def attention_kernel(slot_ref, q_ref, ga_ref, kv_ref, att_ref, gq_ref, sums_ref, sums):
    spans = ROWS // SPAN
    scale = HEAD_DIM ** (-0.5)
    last = lax.axis_index("seq") == NSEQ - 1
    row = lax.broadcasted_iota(jnp.int32, (SPAN, 2 * SPAN), 0)
    col = lax.broadcasted_iota(jnp.int32, (SPAN, 2 * SPAN), 1)
    picked = col == row + (SPAN - 1)
    sums[...] = jnp.zeros_like(sums)

    @pl.loop(0, spans)
    def _(u):
        rows = pl.ds(pl.multiple_of(u * SPAN, SPAN), 2 * SPAN)
        inside = jnp.logical_or(col < SPAN, jnp.logical_not(last & (u == spans - 1)))
        shift = jnp.logical_and(picked, inside).astype(BF16)
        q_all = jnp.dot(shift, q_ref[rows, :], preferred_element_type=F32).astype(BF16)
        g_all = jnp.dot(shift, ga_ref[rows, :], preferred_element_type=F32).astype(BF16)
        slots = [slot_ref[u, j] for j in range(NEIGH)]
        for h in range(W // HEAD_DIM):
            cols = slice(h * HEAD_DIM, (h + 1) * HEAD_DIM)
            q, gr = q_all[:, cols], g_all[:, cols]
            k = jnp.concatenate([kv_ref[s, 0, :, cols] for s in slots], 0)
            v = jnp.concatenate([kv_ref[s, 1, :, cols] for s in slots], 0)
            scores = lax.dot_general(q, k, NT_DIMS, preferred_element_type=F32) * scale
            peak = jnp.max(scores, axis=-1, keepdims=True)
            weights = jnp.exp(scores - peak)
            probs = weights / jnp.sum(weights, axis=-1, keepdims=True)
            probs_low = probs.astype(BF16)
            context = jnp.dot(probs_low, v, preferred_element_type=F32)
            grad_probs = lax.dot_general(gr, v, NT_DIMS, preferred_element_type=F32)
            dot_sum = jnp.sum(grad_probs * probs, axis=-1, keepdims=True)
            grad_scores = (probs * (grad_probs - dot_sum) * scale).astype(BF16)
            grad_q = jnp.dot(grad_scores, k, preferred_element_type=F32)
            grad_k = lax.dot_general(grad_scores, q, TN_DIMS, preferred_element_type=F32)
            grad_v = lax.dot_general(probs_low, gr, TN_DIMS, preferred_element_type=F32)
            here = pl.ds(pl.multiple_of(u * SPAN, SPAN), SPAN)
            att_ref[here, cols] = context.astype(BF16)
            gq_ref[here, cols] = grad_q.astype(BF16)
            for j, s in enumerate(slots):
                part = slice(j * RLEN, (j + 1) * RLEN)
                sums[s, 0, :, cols] += grad_k[part]
                sums[s, 1, :, cols] += grad_v[part]

    @pl.loop(0, sums.shape[0])
    def _(s):
        sums_ref[s] = sums[s].astype(BF16)


class Scatter:
    def __init__(self, grid, order, parts, one, two, three, four, send, recv):
        self.g, self.order, self.parts = grid, order, parts
        self.one, self.two, self.three, self.four = one, two, three, four
        self.msg = Messages(send, recv)
        self.a, self.b = grid.first(order), grid.second(order)

    def part(self, db, da):
        return self.parts.at[wrap(self.b + db, SIDE), wrap(self.a + da, SIDE)]

    def fill(self, db, make):
        b = wrap(self.b + db, SIDE)

        @pl.loop(0, SIDE)
        def _(a):
            self.parts[b, a] = make(self.g.block(self.order, b, a)).astype(BF16)

    def far(self):
        minus, plus = self.g.along_second(self.order, -1), self.g.along_second(self.order, 1)
        self.msg.start(0, self.part(2, 2), self.one.at[0], minus)
        self.msg.start(1, self.part(2, 1), self.one.at[1], plus)
        self.msg.start(2, self.part(2, 0), self.one.at[2], minus)
        self.msg.start(3, self.part(2, 3), self.one.at[3], plus)

    def near_own(self):
        minus, plus = self.g.along_second(self.order, -1), self.g.along_second(self.order, 1)
        self.msg.start(4 + 2, self.part(1, 2), self.two.at[0, 2], plus)
        self.msg.start(8 + 1, self.part(3, 1), self.two.at[1, 1], minus)
        self.msg.start(8 + 3, self.part(3, 3), self.two.at[1, 3], minus)
        self.msg.start(4 + 0, self.part(1, 0), self.two.at[0, 0], plus)

    def add(self, ref, *others):
        total = ref[...].astype(F32)
        for other in others:
            total = total + other[...].astype(F32)
        ref[...] = total.astype(BF16)

    def near_summed(self):
        minus, plus = self.g.along_second(self.order, -1), self.g.along_second(self.order, 1)
        for m, db, da, base, side, peer in (
            (0, 3, 2, 8, 1, minus), (1, 1, 1, 4, 0, plus), (3, 1, 3, 4, 0, plus), (2, 3, 0, 8, 1, minus)
        ):
            self.msg.wait(m, self.one.at[m])
            self.add(self.part(db, da), self.one.at[m])
            self.msg.start(base + da, self.part(db, da), self.two.at[side, da], peer)

    def settle(self, da):
        self.msg.wait(4 + da, self.two.at[0, da])
        self.msg.wait(8 + da, self.two.at[1, da])
        self.add(self.part(0, da), self.two.at[0, da], self.two.at[1, da])

    def first_far(self):
        self.settle(2)
        half = ROWS // 2
        minus, plus = self.g.along_first(self.order, -1), self.g.along_first(self.order, 1)
        self.msg.start(12, self.part(0, 2).at[pl.ds(0, half)], self.three.at[0], minus)
        self.msg.start(13, self.part(0, 2).at[pl.ds(half, half)], self.three.at[1], plus)

    def first_near(self):
        half = ROWS // 2
        minus, plus = self.g.along_first(self.order, -1), self.g.along_first(self.order, 1)
        self.settle(1)
        self.msg.wait(13, self.three.at[1])
        self.add(self.part(0, 1).at[pl.ds(half, half)], self.three.at[1])
        self.msg.start(14, self.part(0, 1), self.four.at[0], plus)
        self.settle(3)
        self.msg.wait(12, self.three.at[0])
        self.add(self.part(0, 3).at[pl.ds(0, half)], self.three.at[0])
        self.msg.start(15, self.part(0, 3), self.four.at[1], minus)

    def end(self, out):
        self.settle(0)
        self.msg.wait(14, self.four.at[0])
        self.msg.wait(15, self.four.at[1])
        total = self.part(0, 0)[...].astype(F32) + self.four[0].astype(F32)
        out[...] = (total + self.four[1].astype(F32)).astype(BF16)


def scatter_kernel(
    att_ref, gq_ref, sums_ref, wq_ref, wk_ref, wv_ref, wo_ref, rows_ref,
    out_ref, gh_ref, ge_ref,
    parts, one, two, three, four, wq, wk, wv, wo, att, gq, att_tok, gq_tok, sums_in, gk, gv,
    send, recv, seq_send, seq_recv, edge_send, edge_recv, local,
):
    g = Grid()
    body, head, last = pl.ds(SPAN, ROWS), pl.ds(0, SPAN), pl.ds(ROWS - SPAN, SPAN)
    copies = [
        pltpu.make_async_copy(src, dst, local.at[i])
        for i, (src, dst) in enumerate(
            (
                (att_ref, att.at[body]), (gq_ref, gq.at[body]), (wo_ref, wo), (wq_ref, wq),
                (wk_ref, wk), (wv_ref, wv), (sums_ref.at[g.seq], sums_in.at[g.seq]),
            )
        )
    ]
    for copy in copies:
        copy.start()
    g.barrier()
    edge = Messages(edge_send, edge_recv)
    edge.start(0, att_ref.at[last], att.at[head], g.along_seq(1))
    edge.start(1, gq_ref.at[last], gq.at[head], g.along_seq(1))
    seq_msg = Messages(seq_send, seq_recv)
    for k in range(1, NSEQ):
        peer = wrap(g.seq + k, NSEQ)
        seq_msg.start(k, sums_ref.at[peer], sums_in.at[g.seq], {"seq": peer})
    for copy in copies:
        copy.wait()
    edge.wait(0, att.at[head])
    edge.wait(1, gq.at[head])

    @pl.when(g.seq == 0)
    def _():
        att[head, :] = jnp.zeros((SPAN, W), BF16)
        gq[head, :] = jnp.zeros((SPAN, W), BF16)

    row = lax.broadcasted_iota(jnp.int32, (SPAN, 2 * SPAN), 0)
    col = lax.broadcasted_iota(jnp.int32, (SPAN, 2 * SPAN), 1)
    shift = (col == row + 1).astype(BF16)

    @pl.loop(0, ROWS // SPAN)
    def _(u):
        rows = pl.ds(pl.multiple_of(u * SPAN, SPAN), 2 * SPAN)
        here = pl.ds(pl.multiple_of(u * SPAN, SPAN), SPAN)
        att_tok[here, :] = jnp.dot(shift, att[rows, :], preferred_element_type=F32).astype(BF16)
        gq_tok[here, :] = jnp.dot(shift, gq[rows, :], preferred_element_type=F32).astype(BF16)

    streams = [
        Scatter(
            g, "zx" if i % 2 == 0 else "xz", parts.at[i], one.at[i], two.at[i], three.at[i],
            four.at[i], send.at[i], recv.at[i],
        )
        for i in range(4)
    ]
    act, enc = streams[:2], streams[2:]

    def out_part(t):
        depth = pl.ds(pl.multiple_of(t * W, W), W)
        return jnp.dot(att_tok[...], wo[:, depth], preferred_element_type=F32)

    def hidden_part(t):
        depth = pl.ds(pl.multiple_of(t * W, W), W)
        return lax.dot_general(gq_tok[...], wq[depth, :], NT_DIMS, preferred_element_type=F32)

    def enc_part(i):
        def make(t):
            depth = pl.ds(pl.multiple_of(t * W, W), W)
            total = lax.dot_general(gk[i], wk[depth, :], NT_DIMS, preferred_element_type=F32)
            return total + lax.dot_general(
                gv[i], wv[depth, :], NT_DIMS, preferred_element_type=F32
            )

        return make

    def launch(pair, makes):
        for s, make in zip(pair, makes):
            s.fill(2, make)
            s.far()
        for s, make in zip(pair, makes):
            s.fill(1, make)
            s.fill(3, make)
            s.near_own()
        for s, make in zip(pair, makes):
            s.fill(0, make)

    launch(act, (out_part, hidden_part))
    for s in act:
        s.near_summed()

    for k in range(1, NSEQ):
        seq_msg.wait(k, sums_in.at[wrap(g.seq - k, NSEQ)])
    targets = [rows_ref[0, j] for j in range(2 * NSEQ)]

    @pl.loop(0, RLEN // 16)
    def _(c):
        tile = pl.ds(pl.multiple_of(c * 16, 16), 16)
        for kind, dest in ((0, gk), (1, gv)):
            for half in range(W // 128):
                cols = slice(half * 128, (half + 1) * 128)
                totals = [jnp.zeros((16, 128), F32) for _ in range(NSEQ)]
                for j in range(2 * NSEQ):
                    value = sums_in[j // 2, j % 2, kind, tile, cols].astype(F32)
                    for n in range(NSEQ):
                        totals[n] = totals[n] + jnp.where(targets[j] == n, value, 0.0)
                for n in range(NSEQ):
                    rows = pl.ds((n % 4) * RLEN + pl.multiple_of(c * 16, 16), 16)
                    dest[n // 4, rows, cols] = totals[n].astype(BF16)

    launch(enc, (enc_part(0), enc_part(1)))
    for s in act:
        s.first_far()
    for s in act:
        s.first_near()
    for s in enc:
        s.near_summed()
    act[0].end(out_ref)
    act[1].end(gh_ref)
    for s in enc:
        s.first_far()
    for s in enc:
        s.first_near()
    enc[0].end(ge_ref.at[pl.ds(0, ROWS)])
    enc[1].end(ge_ref.at[pl.ds(ROWS, ROWS)])
    for s in streams:
        s.msg.finish()
    seq_msg.finish()
    edge.finish()


def params(ident):
    return pltpu.CompilerParams(
        collective_id=ident, has_side_effects=True, vmem_limit_bytes=60 * 1024 * 1024
    )


def shape(*dims, dtype=BF16):
    return jax.ShapeDtypeStruct(dims, dtype)


def per_device(hidden, encoded, w_query, w_key, w_value, w_out, send_rows, read_slot, grad_out):
    dma = pltpu.SemaphoreType.DMA
    weight = pltpu.VMEM((NT * W, W), BF16)
    weight_out = pltpu.VMEM((W, NT * W), BF16)
    block = pltpu.VMEM((ROWS, W), BF16)
    everything = pltpu.VMEM((SIDE, SIDE, ROWS, W), BF16)
    q, ga, kv = pl.pallas_call(
        gather_kernel,
        name="gather_project",
        out_shape=(
            shape(ROWS + SPAN, W), shape(ROWS + SPAN, W), shape(NSEQ, 2, 2, RLEN, W),
        ),
        in_specs=[ANY] * 7 + [SM],
        out_specs=(ANY, ANY, ANY),
        scratch_shapes=[
            everything, everything, everything, everything,
            weight, weight, weight, weight_out,
            pltpu.VMEM((2, ROWS, W), F32), pltpu.VMEM((2, ROWS, W), F32),
            pltpu.VMEM((NSEQ, 2, RLEN, W), BF16), pltpu.VMEM((NSEQ, 2, 2, RLEN, W), BF16),
            block, block,
            dma((4, 16)), dma((4, 16)), dma((NSEQ,)), dma((NSEQ,)), dma((2,)), dma((2,)), dma((9,)),
        ],
        compiler_params=params(0),
    )(
        encoded.reshape(2 * ROWS, W), hidden, grad_out, w_query, w_key, w_value, w_out, send_rows,
    )
    att, gq, sums = pl.pallas_call(
        attention_kernel,
        name="attention",
        out_shape=(shape(ROWS, W), shape(ROWS, W), shape(2 * NSEQ, 2, RLEN, W)),
        in_specs=[SM, VM, VM, VM],
        out_specs=(VM, VM, VM),
        scratch_shapes=[pltpu.VMEM((2 * NSEQ, 2, RLEN, W), F32)],
        compiler_params=pltpu.CompilerParams(vmem_limit_bytes=60 * 1024 * 1024),
    )(read_slot, q, ga, kv.reshape(2 * NSEQ, 2, RLEN, W))
    out, gh, ge = pl.pallas_call(
        scatter_kernel,
        name="project_scatter",
        out_shape=(shape(ROWS, W), shape(ROWS, W), shape(2 * ROWS, W)),
        in_specs=[ANY] * 7 + [SM],
        out_specs=(VM, VM, VM),
        scratch_shapes=[
            pltpu.VMEM((4, SIDE, SIDE, ROWS, W), BF16),
            pltpu.VMEM((4, 4, ROWS, W), BF16),
            pltpu.VMEM((4, 2, 4, ROWS, W), BF16),
            pltpu.VMEM((4, 2, ROWS // 2, W), BF16),
            pltpu.VMEM((4, 2, ROWS, W), BF16),
            weight, weight, weight, weight_out,
            pltpu.VMEM((ROWS + SPAN, W), BF16), pltpu.VMEM((ROWS + SPAN, W), BF16),
            block, block,
            pltpu.VMEM((NSEQ, 2, 2, RLEN, W), BF16),
            pltpu.VMEM((2, ROWS, W), BF16), pltpu.VMEM((2, ROWS, W), BF16),
            dma((4, 16)), dma((4, 16)), dma((NSEQ,)), dma((NSEQ,)), dma((2,)), dma((2,)), dma((9,)),
        ],
        compiler_params=params(1),
    )(
        att, gq, sums.reshape(NSEQ, 2, 2, RLEN, W), w_query, w_key, w_value, w_out, send_rows,
    )
    return out, gh, ge.reshape(encoded.shape)


def solution(mesh):
    placed = (
        P("seq", "tensor"),
        P("seq", None, "tensor"),
        P(None, "tensor"),
        P(None, "tensor"),
        P(None, "tensor"),
        P("tensor", None),
        P("seq", None),
        P("seq", None),
        P("seq", "tensor"),
    )
    return jax.shard_map(
        per_device,
        mesh=mesh,
        in_specs=placed,
        out_specs=(P("seq", "tensor"), P("seq", "tensor"), P("seq", None, "tensor")),
        check_vma=False,
    )
```

time: 490 us -> 226 us (0.46)
  waiting for transfers between devices: 290 us -> 0 us
  Pallas kernels: 0 us -> 218 us
  matrix products: 89.3 us -> 0 us
  local copies, waits for them, and re-layouts: 43.6 us -> 6.55 us
  blocking collectives: 32.7 us -> 0 us
  between operations: 14.4 us -> 0.65 us
  other arithmetic: 10.8 us -> 0 us
  starting transfers between devices: 7.7 us -> 0 us
    pallas_call x0 -> x3, Pallas kernels: none -> 218 us  [the longest x1 103 us: per_device(): pl.pallas_call(scatter_kernel, name='project_scatter', out_shape=(shape(R...]
    all_gather x3 -> x0, waiting for transfers between devices: 163 us -> none  [the longest x1 81 us: per_device(): piece = lax.all_gather(encoded, 'tensor', axis=2, tiled=True)]
    reduce_scatter x3 -> x0, waiting for transfers between devices: 125 us -> none  [the longest x1 88.2 us: per_device(): lax.psum_scatter(partial_enc.astype(jnp.bfloat16), 'tensor', scatter_dime...]
    dot_general x17 -> x0, matrix products: 89.3 us -> none  [the longest x1 11.8 us: per_device(): lax.dot_general(grad_value_rows, w_value, contract, preferred_element_typ...]
    all_to_all x1 -> x0, blocking collectives: 32.7 us -> none  [per_device(): lax.all_to_all(slot_grads, 'seq', split_axis=0, concat_axis=0, tiled=True)]
    slice x12 -> x0, local copies, waits for them, and re-layouts: 18.8 us -> none  [the longest x2 6.32 us: per_device(): read_keys = grad_k[1:].at[spans_here - 1].add(edge_grads[0])]
    gather x3 -> x0, local copies, waits for them, and re-layouts: 7.85 us -> none  [the longest x2 4.27 us: per_device(): outgoing = jnp.stack([keys[safe_rows], values[safe_rows]], 1)]
    reshape x3 -> x0, local copies, waits for them, and re-layouts: 5.6 us -> none  [the longest x1 2.76 us: per_device(): read_keys.reshape(spans_here * NEIGH, read_flat)]
  transfers between devices with their start and end apart: 9 -> 0, of which waited for: 5 -> 0; matrix products, arithmetic and copies ran while one was open for 26% -> 0% of each run, Pallas kernels for 0% -> 0%
where the time goes in v1:
time: 226 us; the launch traced here: 225 us
  Pallas kernels  218 us (96%)
  local copies, waits for them, and re-layouts  6.55 us (3%)
    pallas_call x1, Pallas kernels, per_device(): pl.pallas_call(scatter_kernel, name='project_scatter', out_shape=(shape(R...  103 us
    pallas_call x1, Pallas kernels, per_device(): pl.pallas_call(gather_kernel, name='gather_project', out_shape=(shape(ROW...  100 us
    pallas_call x1, Pallas kernels, per_device(): pl.pallas_call(attention_kernel, name='attention', out_shape=(shape(ROWS,...  14.5 us
    unnamed x4, local copies, waits for them, and re-layouts  6.55 us

profile of v1, /device:TPU:0, one launch (start us, length us, event | category | flops | bytes accessed | tf_op | source)
XLA Modules:
  0.0 225.2 jit_solution(1225569790443871137)
XLA Ops:
  0.6 1.3 copy.12.slot_ref
  2.0 100.2 %gather_project.1 = (bf16[576,256]{1,0:T(8,128)(2,1)}, bf16[576,256]{1,0:T(8,128)(2,1)}, bf16[8,2,2,128,256]{4,3,2,1,0:T(8,128)(2,1)}) custom-call(bf16[1024,256]{1,0:T(8,128)(2,1)} %bitcast.6, bf16[512,256]{1,0:T(8,128)(2,1)} %hid_ref.1, bf16[512,256]{1,0:T(8,128)(2,1)} %gout_ref.1, bf16[4096,256]{1,0:T(8,128)(2,1)} %wq_ref.3, bf16[4096,256]{1,0:T(8,128)(2,1)} %wk_ref.3, ...), custom_call_target="tpu_custom_call" | custom-call | tf_op jit(solution)/shard_map/gather_project/pallas_call | solution.py:577
  102.1 14.5 %attention.1 = (bf16[512,256]{1,0:T(8,128)(2,1)}, bf16[512,256]{1,0:T(8,128)(2,1)}, bf16[16,2,128,256]{3,2,1,0:T(8,128)(2,1)}) custom-call(s32[8,2]{1,0:T(8,128)} %copy.12.slot_ref, bf16[576,256]{1,0:T(8,128)(2,1)} %get-tuple-element.12.q_ref, bf16[576,256]{1,0:T(8,128)(2,1)} %get-tuple-element.13.ga_ref, bf16[16,2,128,256]{3,2,1,0:T(8,128)(2,1)} %bitcast.4), custom_call_target="tpu_custom_call" | custom-call | tf_op jit(solution)/shard_map/attention/pallas_call | solution.py:597
  116.6 103.4 %project_scatter.1 = (bf16[512,256]{1,0:T(8,128)(2,1)}, bf16[512,256]{1,0:T(8,128)(2,1)}, bf16[1024,256]{1,0:T(8,128)(2,1)}) custom-call(bf16[512,256]{1,0:T(8,128)(2,1)} %get-tuple-element.15.att_ref, bf16[512,256]{1,0:T(8,128)(2,1)} %get-tuple-element.16.gq_ref, bf16[8,2,2,128,256]{4,3,2,1,0:T(8,128)(2,1)} %bitcast.5, bf16[4096,256]{1,0:T(8,128)(2,1)} %wq_ref.3, ...), custom_call_target="tpu_custom_call" | custom-call | tf_op jit(solution)/shard_map/project_scatter/pallas_call | solution.py:606
  220.0 1.7 copy.16
  221.7 1.7 copy.17
  223.4 1.9 copy.18

commit v2 on v0

v2 whole, which is shorter than its diff:
```python
import functools

import jax
import jax.numpy as jnp
from jax import lax
from jax.experimental import pallas as pl
from jax.experimental.pallas import tpu as pltpu
from jax.sharding import PartitionSpec as P

SPAN = 64
NEIGH = 2
RLEN = 128
HEAD_DIM = 128
NSEQ = 8
SIDE = 4
NT = SIDE * SIDE
W = 256
ROWS = 512
Q = ROWS // SIDE
EQ = 2 * ROWS // SIDE
MESH = pl.DeviceIdType.MESH
ANY = pl.BlockSpec(memory_space=pl.ANY)
VM = pl.BlockSpec(memory_space=pltpu.VMEM)
SM = pl.BlockSpec(memory_space=pltpu.SMEM)
F32 = jnp.float32
BF16 = jnp.bfloat16
NT_DIMS = (((1,), (1,)), ((), ()))
TN_DIMS = (((0,), (0,)), ((), ()))


def wrap(value, count):
    return lax.rem(value + count, count)


class Grid:
    def __init__(self):
        self.seq = lax.axis_index("seq")
        tensor = lax.axis_index("tensor")
        self.z = lax.div(tensor, SIDE)
        self.x = lax.rem(tensor, SIDE)
        self.y = lax.div(self.seq, 2)
        self.core = lax.rem(self.seq, 2)

    def at(self, axis):
        return self.z if axis == "z" else self.x

    def along(self, axis, step):
        if axis == "z":
            return {"tensor": wrap(self.z + step, SIDE) * SIDE + self.x}
        if axis == "x":
            return {"tensor": self.z * SIDE + wrap(self.x + step, SIDE)}
        if axis == "y":
            return {"seq": wrap(self.y + step, SIDE) * 2 + self.core}
        if axis == "core":
            return {"seq": self.y * 2 + (1 - self.core)}
        return {"seq": wrap(self.seq + step, NSEQ)}

    def barrier(self):
        sem = pltpu.get_barrier_semaphore()
        peers = [self.along(axis, k) for axis in "zx" for k in range(1, SIDE)]
        peers += [self.along("seq", k) for k in range(1, NSEQ)]
        for peer in peers:
            pl.semaphore_signal(sem, inc=1, device_id=peer, device_id_type=MESH)
        pl.semaphore_wait(sem, len(peers))


class Messages:
    def __init__(self, send, recv):
        self.send, self.recv, self.sent, self.used = send, recv, [], 0

    def block(self, count):
        self.used += count
        return self.used - count

    def start(self, m, src, dst, peer):
        copy = pltpu.make_async_remote_copy(
            src_ref=src,
            dst_ref=dst,
            send_sem=self.send.at[m],
            recv_sem=self.recv.at[m],
            device_id=peer,
            device_id_type=MESH,
        )
        copy.start()
        self.sent.append(copy)

    def wait(self, m, dst):
        pltpu.make_async_copy(dst, dst, self.recv.at[m]).wait()

    def finish(self):
        for copy in self.sent:
            copy.wait_send()
        self.sent = []


class Gather:
    def __init__(self, grid, msg, cut, ring, own, buf):
        self.g, self.msg, self.cut, self.ring, self.own, self.buf = grid, msg, cut, ring, own, buf
        self.n = buf.shape[2]
        self.i, self.j = grid.at(cut), grid.at(ring)
        self.base = msg.block(15)

    def slot(self, dj, di):
        return self.buf.at[wrap(self.j + dj, SIDE), wrap(self.i + di, SIDE)]

    def quarter(self, di):
        start = wrap(self.i + di, SIDE) * self.n
        return self.own.at[pl.ds(pl.multiple_of(start, self.n), self.n)]

    def swap(self):
        for k in (1, 3, 2):
            peer = self.g.along(self.cut, k)
            self.msg.start(self.base + k - 1, self.quarter(k), self.slot(0, 0), peer)

    def spread(self, di):
        src = self.quarter(0) if di == 0 else self.slot(0, di)
        if di:
            self.msg.wait(self.base + SIDE - di - 1, src)
        for n, step in enumerate((1, -1)):
            self.msg.start(
                self.base + 3 + 2 * di + n, src, self.slot(0, di), self.g.along(self.ring, step)
            )

    def forward(self, di):
        ahead = di in (0, 1)
        self.msg.wait(self.base + 3 + 2 * di, self.slot(3, di))
        self.msg.wait(self.base + 4 + 2 * di, self.slot(1, di))
        block = self.slot(3 if ahead else 1, di)
        self.msg.start(
            self.base + 11 + di, block, block, self.g.along(self.ring, 1 if ahead else -1)
        )

    def settle(self):
        for di in range(SIDE):
            self.msg.wait(self.base + 11 + di, self.slot(2, di))


class Weight:
    def __init__(self, grid, msg, cut, own, full, shared, wide):
        self.g, self.msg, self.cut, self.own, self.full = grid, msg, cut, own, full
        self.shared, self.wide = shared, wide
        self.i = grid.at(cut)
        self.base = msg.block(17)
        self.half = NT * W // 2
        self.n = self.half // SIDE if shared else self.half

    def cutout(self, ref, start, size):
        rows = pl.ds(pl.multiple_of(start, W), size)
        return ref.at[:, rows] if self.wide else ref.at[rows]

    def region(self, core):
        return core * self.half, self.half

    def chunk(self, dy=0):
        if not self.shared:
            return self.region(self.g.core)
        return self.g.core * self.half + wrap(self.g.y + dy, SIDE) * self.n, self.n

    def piece(self, e, where, part=None):
        start, size = where
        if part is not None:
            size = size // 2
            start = start + part * size
        return self.cutout(self.full.at[wrap(self.i + e, SIDE)], start, size)

    def start(self):
        mine = self.cutout(self.own, *self.chunk())
        for n, step in enumerate((1, -1)):
            self.msg.start(
                self.base + n, mine, self.piece(0, self.chunk()), self.g.along(self.cut, step)
            )

    def share(self, e):
        if self.shared:
            first = {3: 4, 1: 6, 2: 8}[e]
            block = self.piece(e, self.chunk())
            for n, step in enumerate((1, -1)):
                self.msg.start(self.base + first + n, block, block, self.g.along("y", step))
        else:
            self.swap_cores(e)

    def swap_cores(self, e):
        block = self.piece(e, self.region(self.g.core))
        self.msg.start(self.base + 14 + {3: 0, 1: 1, 2: 2}[e], block, block, self.g.along("core", 1))

    def near(self):
        here = self.chunk()
        self.msg.wait(self.base, self.piece(3, here))
        part = self.piece(3, here, 0)
        self.msg.start(self.base + 2, part, part, self.g.along(self.cut, 1))
        self.msg.wait(self.base + 1, self.piece(1, here))
        part = self.piece(1, here, 1)
        self.msg.start(self.base + 3, part, part, self.g.along(self.cut, -1))
        self.share(3)
        self.share(1)

    def far(self):
        here = self.chunk()
        self.msg.wait(self.base + 2, self.piece(2, here, 0))
        self.msg.wait(self.base + 3, self.piece(2, here, 1))
        self.share(2)

    def shared_near(self):
        up, down = self.chunk(-1), self.chunk(1)
        for e, first in ((3, 4), (1, 6)):
            self.msg.wait(self.base + first, self.piece(e, up))
            self.msg.wait(self.base + first + 1, self.piece(e, down))
        block = self.piece(3, up)
        self.msg.start(self.base + 10, block, block, self.g.along("y", 1))
        block = self.piece(1, down)
        self.msg.start(self.base + 11, block, block, self.g.along("y", -1))

    def shared_far(self):
        up, down = self.chunk(-1), self.chunk(1)
        self.msg.wait(self.base + 8, self.piece(2, up))
        self.msg.wait(self.base + 9, self.piece(2, down))
        block = self.piece(2, up, 0)
        self.msg.start(self.base + 12, block, block, self.g.along("y", 1))
        block = self.piece(2, down, 1)
        self.msg.start(self.base + 13, block, block, self.g.along("y", -1))

    def shared_end(self):
        across = self.chunk(2)
        self.msg.wait(self.base + 10, self.piece(3, across))
        self.swap_cores(3)
        self.msg.wait(self.base + 11, self.piece(1, across))
        self.swap_cores(1)
        self.msg.wait(self.base + 12, self.piece(2, across, 0))
        self.msg.wait(self.base + 13, self.piece(2, across, 1))
        self.swap_cores(2)

    def ready(self, e):
        if e:
            m = self.base + 14 + {3: 0, 1: 1, 2: 2}[e]
            self.msg.wait(m, self.piece(e, self.region(1 - self.g.core)))


def lanes(blocks):
    return jnp.concatenate(blocks, 1)


def gather_kernel(
    enc_ref, hid_ref, gout_ref, wq_ref, wk_ref, wv_ref, wo_ref, rows_ref,
    q_ref, ga_ref, kv_ref, wq_out, wk_out, wv_out, wo_out,
    enc_all, hid_all, gout_all, wq, wk, wv, wo, kv_send, q_send, ga_send, own_k, own_v, stage, q_low, ga_low,
    send, recv, local,
):
    g = Grid()
    msg = Messages(send, recv)
    used = [0]

    def copy(src, dst):
        used[0] += 1
        return pltpu.make_async_copy(src, dst, local.at[used[0] - 1])

    enc = Gather(g, msg, "x", "z", enc_ref, enc_all)
    hid = Gather(g, msg, "z", "x", hid_ref, hid_all)
    gout = Gather(g, msg, "z", "x", gout_ref, gout_all)
    w_key = Weight(g, msg, "x", wk_ref, wk, True, False)
    w_value = Weight(g, msg, "x", wv_ref, wv, False, False)
    w_query = Weight(g, msg, "z", wq_ref, wq, True, False)
    w_out = Weight(g, msg, "z", wo_ref, wo, False, True)
    loads = [copy(s.quarter(0), s.slot(0, 0)) for s in (enc, hid, gout)]
    loads += [copy(w.own, w.full.at[w.i]) for w in (w_key, w_value, w_query, w_out)]
    g.barrier()
    enc.swap()
    hid.swap()
    gout.swap()
    w_key.start()
    enc.spread(0)
    w_query.start()
    w_value.start()
    for load in loads:
        load.start()
    for di in (3, 1, 2):
        enc.spread(di)
    w_out.start()
    for di in (0, 3, 1):
        enc.forward(di)
    w_key.near()
    w_key.far()
    enc.forward(2)
    w_query.near()
    w_query.far()
    for s in (hid, gout):
        for di in (0, 3, 1, 2):
            s.spread(di)
    w_key.shared_near()
    w_key.shared_far()
    enc.settle()
    w_value.near()
    w_key.shared_end()
    w_query.shared_near()
    w_query.shared_far()
    for load in loads:
        load.wait()

    keep = []
    out_base = msg.block(12)

    def columns(s, w, e):
        w.ready(e)
        at = wrap(w.i + e, SIDE)
        total = None
        for n in range(SIDE):
            if s.ring == "z":
                left = lanes([s.buf[n, k] for k in range(SIDE)])
            else:
                left = lanes([s.buf[k, n] for k in range(SIDE)])
            depth = pl.ds(n * SIDE * W, SIDE * W)
            if w.wide:
                term = lax.dot_general(
                    left, w.full[at, :, depth], NT_DIMS, preferred_element_type=F32
                )
            else:
                term = jnp.dot(left, w.full[at, depth, :], preferred_element_type=F32)
            total = term if total is None else total + term
        return total.astype(BF16)

    def project(s, w, e, kind, dst, sender):
        value = columns(s, w, e)
        shaped = value.reshape(sender.shape[1:])
        if e == 0:
            dst[...] = shaped
        else:
            sender[e] = shaped
            msg.start(out_base + 3 * kind + e - 1, sender.at[e], dst, g.along(s.cut, e))

    def arrived(s, kind, dst_of):
        for e in range(1, SIDE):
            msg.wait(out_base + 3 * kind + e - 1, dst_of(wrap(s.i - e, SIDE)))

    per = SPAN * 4 // RLEN

    def kv_rows(kind):
        return lambda i: (own_k, own_v)[kind].at[pl.ds(i * per, per)]

    for e in (0, 3, 1, 2):
        project(enc, w_key, e, 0, kv_rows(0)(g.x), kv_send.at[0])
    w_value.far()
    w_out.near()
    for e in (0, 3, 1, 2):
        project(enc, w_value, e, 1, kv_rows(1)(g.x), kv_send.at[1])

    seq_base = msg.block(2 * NSEQ)

    def exchange(kind):
        arrived(enc, kind, kv_rows(kind))

        @pl.loop(0, NSEQ)
        def _(r):
            for s in range(2):
                stage[kind, r, s] = (own_k, own_v)[kind][jnp.maximum(rows_ref[0, 2 * r + s], 0)]

        for k in range(1, NSEQ):
            peer = wrap(g.seq + k, NSEQ)
            msg.start(
                seq_base + NSEQ * kind + k, stage.at[kind, peer], kv_ref.at[kind, g.seq], {"seq": peer}
            )
        own = copy(stage.at[kind, g.seq], kv_ref.at[kind, g.seq])
        own.start()
        keep.append(own)

    exchange(0)
    exchange(1)
    w_query.shared_end()
    w_out.far()
    for s in (hid, gout):
        for di in (0, 3, 1, 2):
            s.forward(di)
    for s in (hid, gout):
        s.settle()

    def rows_of(ref):
        return lambda i: ref.at[pl.ds(pl.multiple_of(i * Q, Q), Q)]

    for e in (0, 3, 1, 2):
        project(hid, w_query, e, 2, rows_of(q_low)(g.z), q_send)
    for e in (0, 3, 1, 2):
        project(gout, w_out, e, 3, rows_of(ga_low)(g.z), ga_send)
    weights_out = [
        copy(w.full, out)
        for w, out in ((w_key, wk_out), (w_value, wv_out), (w_query, wq_out), (w_out, wo_out))
    ]
    for c in weights_out:
        c.start()
    edge = msg.block(2)
    head, tail, body = pl.ds(0, SPAN), pl.ds(ROWS, SPAN), pl.ds(0, ROWS)
    for kind, (s, low, ref) in enumerate(((hid, q_low, q_ref), (gout, ga_low, ga_ref))):
        arrived(s, 2 + kind, rows_of(low))
        msg.start(edge + kind, low.at[head], ref.at[tail], g.along("seq", -1))
        own = copy(low, ref.at[body])
        own.start()
        keep.append(own)
    for kind in range(2):
        for k in range(1, NSEQ):
            msg.wait(seq_base + NSEQ * kind + k, kv_ref.at[kind, wrap(g.seq - k, NSEQ)])
    msg.wait(edge, q_ref.at[tail])
    msg.wait(edge + 1, ga_ref.at[tail])
    msg.finish()
    for c in keep + weights_out:
        c.wait()


def attention_kernel(slot_ref, q_ref, ga_ref, kv_ref, att_ref, gq_ref, sums_ref, sums):
    spans = ROWS // SPAN
    scale = HEAD_DIM ** (-0.5)
    last = lax.axis_index("seq") == NSEQ - 1
    row = lax.broadcasted_iota(jnp.int32, (SPAN, 2 * SPAN), 0)
    col = lax.broadcasted_iota(jnp.int32, (SPAN, 2 * SPAN), 1)
    picked = col == row + (SPAN - 1)
    sums[...] = jnp.zeros_like(sums)

    @pl.loop(0, spans)
    def _(u):
        rows = pl.ds(pl.multiple_of(u * SPAN, SPAN), 2 * SPAN)
        inside = jnp.logical_or(col < SPAN, jnp.logical_not(last & (u == spans - 1)))
        shift = jnp.logical_and(picked, inside).astype(BF16)
        q_all = jnp.dot(shift, q_ref[rows, :], preferred_element_type=F32).astype(BF16)
        g_all = jnp.dot(shift, ga_ref[rows, :], preferred_element_type=F32).astype(BF16)
        slots = [slot_ref[u, j] for j in range(NEIGH)]
        for h in range(W // HEAD_DIM):
            cols = slice(h * HEAD_DIM, (h + 1) * HEAD_DIM)
            q, gr = q_all[:, cols], g_all[:, cols]
            k = jnp.concatenate([kv_ref[0, s, :, cols] for s in slots], 0)
            v = jnp.concatenate([kv_ref[1, s, :, cols] for s in slots], 0)
            scores = lax.dot_general(q, k, NT_DIMS, preferred_element_type=F32) * scale
            peak = jnp.max(scores, axis=-1, keepdims=True)
            weights = jnp.exp(scores - peak)
            probs = weights / jnp.sum(weights, axis=-1, keepdims=True)
            probs_low = probs.astype(BF16)
            context = jnp.dot(probs_low, v, preferred_element_type=F32)
            grad_probs = lax.dot_general(gr, v, NT_DIMS, preferred_element_type=F32)
            dot_sum = jnp.sum(grad_probs * probs, axis=-1, keepdims=True)
            grad_scores = (probs * (grad_probs - dot_sum) * scale).astype(BF16)
            grad_q = jnp.dot(grad_scores, k, preferred_element_type=F32)
            grad_k = lax.dot_general(grad_scores, q, TN_DIMS, preferred_element_type=F32)
            grad_v = lax.dot_general(probs_low, gr, TN_DIMS, preferred_element_type=F32)
            here = pl.ds(pl.multiple_of(u * SPAN, SPAN), SPAN)
            att_ref[here, cols] = context.astype(BF16)
            gq_ref[here, cols] = grad_q.astype(BF16)
            for j, s in enumerate(slots):
                part = slice(j * RLEN, (j + 1) * RLEN)
                sums[s, 0, :, cols] += grad_k[part]
                sums[s, 1, :, cols] += grad_v[part]

    @pl.loop(0, sums.shape[0])
    def _(s):
        sums_ref[s] = sums[s].astype(BF16)


class Scatter:
    def __init__(self, grid, msg, cut, ring, own, got, parts, one, two):
        self.g, self.msg, self.cut, self.ring = grid, msg, cut, ring
        self.own, self.got, self.parts, self.one, self.two = own, got, parts, one, two
        self.i, self.j = grid.at(cut), grid.at(ring)
        self.base = msg.block(12)

    def swap(self):
        for k in (1, 3, 2):
            peer = wrap(self.i + k, SIDE)
            self.msg.start(
                self.base + k - 1, self.own.at[peer], self.got.at[self.i], self.g.along(self.cut, k)
            )
        self.got[self.i] = self.own[self.i]

    def swapped(self):
        for k in (1, 3, 2):
            self.msg.wait(self.base + k - 1, self.got.at[wrap(self.i - k, SIDE)])

    def part(self, dj, where=None):
        block = self.parts.at[wrap(self.j + dj, SIDE)]
        return block if where is None else block.at[pl.ds(2 * where, 2)]

    def fill(self, dj, make):
        j = wrap(self.j + dj, SIDE)

        @pl.loop(0, SIDE)
        def _(i):
            t = j * SIDE + i if self.ring == "z" else i * SIDE + j
            self.parts[j, i] = make(t).astype(BF16)

    def far(self):
        self.msg.start(self.base + 3, self.part(2, 0), self.one.at[0], self.g.along(self.ring, -1))
        self.msg.start(self.base + 4, self.part(2, 1), self.one.at[1], self.g.along(self.ring, 1))

    def to_plus(self, where):
        self.msg.start(
            self.base + 5 + where, self.part(1, where), self.two.at[0, pl.ds(2 * where, 2)],
            self.g.along(self.ring, 1),
        )

    def to_minus(self, where):
        self.msg.start(
            self.base + 7 + where, self.part(3, where), self.two.at[1, pl.ds(2 * where, 2)],
            self.g.along(self.ring, -1),
        )

    def add(self, ref, *others):
        total = ref[...].astype(F32)
        for other in others:
            total = total + other[...].astype(F32)
        ref[...] = total.astype(BF16)

    def near(self):
        self.msg.wait(self.base + 3, self.one.at[0])
        self.add(self.part(3, 0), self.one.at[0])
        self.to_minus(0)
        self.msg.wait(self.base + 4, self.one.at[1])
        self.add(self.part(1, 1), self.one.at[1])
        self.to_plus(1)

    def end(self, out):
        n = self.parts.shape[2]
        for where in (1, 0):
            half = pl.ds(2 * where, 2)
            self.msg.wait(self.base + 5 + where, self.two.at[0, half])
            self.msg.wait(self.base + 7 + where, self.two.at[1, half])
            self.add(self.part(0, where), self.two.at[0, half], self.two.at[1, half])

        def rows(i):
            return out.at[pl.ds(pl.multiple_of(i * n, n), n)]

        for k in (1, 3, 2):
            self.msg.start(
                self.base + 8 + k, self.part(0).at[wrap(self.i + k, SIDE)], rows(self.i),
                self.g.along(self.cut, k),
            )
        rows(self.i)[...] = self.part(0)[self.i]
        return rows

    def back(self, rows):
        for k in range(1, SIDE):
            self.msg.wait(self.base + 8 + k, rows(wrap(self.i - k, SIDE)))


def scatter_kernel(
    att_ref, gq_ref, sums_ref, wq_ref, wk_ref, wv_ref, wo_ref, rows_ref,
    out_ref, gh_ref, ge_ref,
    parts, parts_enc, one, one_enc, two, two_enc, wq, wk, wv, wo, att, gq, tok, got, sums_in, gkv, gkv_got,
    send, recv, local,
):
    g = Grid()
    msg = Messages(send, recv)
    body, head, last = pl.ds(SPAN, ROWS), pl.ds(0, SPAN), pl.ds(ROWS - SPAN, SPAN)
    copies = [
        pltpu.make_async_copy(src, dst, local.at[i])
        for i, (src, dst) in enumerate(
            (
                (att_ref, att.at[body]), (gq_ref, gq.at[body]), (sums_ref.at[g.seq], sums_in.at[g.seq]),
                (wo_ref, wo), (wq_ref, wq), (wk_ref, wk), (wv_ref, wv),
            )
        )
    ]
    for c in copies:
        c.start()
    g.barrier()
    edge, seq_base = msg.block(2), msg.block(NSEQ)
    msg.start(edge, att_ref.at[last], att.at[head], g.along("seq", 1))
    msg.start(edge + 1, gq_ref.at[last], gq.at[head], g.along("seq", 1))
    for k in range(1, NSEQ):
        peer = wrap(g.seq + k, NSEQ)
        msg.start(seq_base + k, sums_ref.at[peer], sums_in.at[g.seq], {"seq": peer})
    streams = [
        Scatter(g, msg, "z", "x", tok.at[i], got.at[i], parts.at[i], one.at[i], two.at[i])
        for i in range(2)
    ]
    enc = Scatter(g, msg, "x", "z", gkv, gkv_got, parts_enc, one_enc, two_enc)
    copies[0].wait()
    copies[1].wait()
    msg.wait(edge, att.at[head])
    msg.wait(edge + 1, gq.at[head])

    @pl.when(g.seq == 0)
    def _():
        att[head, :] = jnp.zeros((SPAN, W), BF16)
        gq[head, :] = jnp.zeros((SPAN, W), BF16)

    row = lax.broadcasted_iota(jnp.int32, (Q, Q + SPAN), 0)
    col = lax.broadcasted_iota(jnp.int32, (Q, Q + SPAN), 1)
    shift = (col == row + 1).astype(BF16)
    for kind, src in ((0, att), (1, gq)):
        for n in range(SIDE):
            moved = jnp.dot(shift, src[n * Q : (n + 1) * Q + SPAN, :], preferred_element_type=F32)
            tok[kind, n] = moved.astype(BF16)
        streams[kind].swap()

    def out_part(t):
        depth = pl.ds(pl.multiple_of(t * W, W), W)
        return sum(
            jnp.dot(got[0, i], wo[i, :, depth], preferred_element_type=F32) for i in range(SIDE)
        )

    def hidden_part(t):
        depth = pl.ds(pl.multiple_of(t * W, W), W)
        return sum(
            lax.dot_general(got[1, i], wq[i, depth, :], NT_DIMS, preferred_element_type=F32)
            for i in range(SIDE)
        )

    def enc_part(t):
        depth = pl.ds(pl.multiple_of(t * W, W), W)
        total = None
        for kind, w in ((0, wk), (1, wv)):
            for i in range(SIDE):
                term = lax.dot_general(
                    gkv_got[i, kind], w[i, depth, :], NT_DIMS, preferred_element_type=F32
                )
                total = term if total is None else total + term
        return total

    def launch(s, make):
        s.swapped()
        s.fill(2, make)
        s.far()
        s.fill(1, make)
        s.to_plus(0)
        s.fill(3, make)
        s.to_minus(1)
        s.fill(0, make)

    copies[3].wait()
    launch(streams[0], out_part)
    copies[4].wait()
    launch(streams[1], hidden_part)
    for s in streams:
        s.near()
    copies[2].wait()
    for k in range(1, NSEQ):
        msg.wait(seq_base + k, sums_in.at[wrap(g.seq - k, NSEQ)])
    targets = [rows_ref[0, j] for j in range(2 * NSEQ)]
    per = EQ // RLEN

    @pl.loop(0, RLEN // 16)
    def _(c):
        tile = pl.ds(pl.multiple_of(c * 16, 16), 16)
        for kind in range(2):
            for half in range(W // 128):
                cols = slice(half * 128, (half + 1) * 128)
                totals = [jnp.zeros((16, 128), F32) for _ in range(NSEQ)]
                for j in range(2 * NSEQ):
                    value = sums_in[j // 2, j % 2, kind, tile, cols].astype(F32)
                    for n in range(NSEQ):
                        totals[n] = totals[n] + jnp.where(targets[j] == n, value, 0.0)
                for n in range(NSEQ):
                    rows = pl.ds((n % per) * RLEN + pl.multiple_of(c * 16, 16), 16)
                    gkv[n // per, kind, rows, cols] = totals[n].astype(BF16)

    enc.swap()
    ends = [s.end(out) for s, out in zip(streams, (out_ref, gh_ref))]
    copies[5].wait()
    copies[6].wait()
    launch(enc, enc_part)
    enc.near()
    end = enc.end(ge_ref)
    for s, rows in zip(streams, ends):
        s.back(rows)
    enc.back(end)
    msg.finish()


def params(ident):
    return pltpu.CompilerParams(
        collective_id=ident, has_side_effects=True, vmem_limit_bytes=60 * 1024 * 1024
    )


def shape(*dims, dtype=BF16):
    return jax.ShapeDtypeStruct(dims, dtype)


def per_device(hidden, encoded, w_query, w_key, w_value, w_out, send_rows, read_slot, grad_out):
    dma = pltpu.SemaphoreType.DMA
    weight = pltpu.VMEM((SIDE, NT * W, W), BF16)
    weight_out = pltpu.VMEM((SIDE, W, NT * W), BF16)
    block = pltpu.VMEM((ROWS, W), BF16)
    quarters = pltpu.VMEM((SIDE, Q, W), BF16)
    tall = shape(SIDE, NT * W, W)
    q, ga, kv, wq, wk, wv, wo = pl.pallas_call(
        gather_kernel,
        name="gather_project",
        out_shape=(
            shape(ROWS + SPAN, W), shape(ROWS + SPAN, W), shape(2, NSEQ, 2, RLEN, W),
            tall, tall, tall, shape(SIDE, W, NT * W),
        ),
        in_specs=[ANY] * 7 + [SM],
        out_specs=(ANY,) * 7,
        scratch_shapes=[
            pltpu.VMEM((SIDE, SIDE, EQ, W), BF16),
            pltpu.VMEM((SIDE, SIDE, Q, W), BF16), pltpu.VMEM((SIDE, SIDE, Q, W), BF16),
            weight, weight, weight, weight_out,
            pltpu.VMEM((2, SIDE, EQ // RLEN, RLEN, W), BF16), quarters, quarters,
            pltpu.VMEM((NSEQ, RLEN, W), BF16), pltpu.VMEM((NSEQ, RLEN, W), BF16),
            pltpu.VMEM((2, NSEQ, 2, RLEN, W), BF16),
            block, block,
            dma((144,)), dma((144,)), dma((16,)),
        ],
        compiler_params=params(0),
    )(
        encoded.reshape(2 * ROWS, W), hidden, grad_out, w_query, w_key, w_value, w_out, send_rows,
    )
    att, gq, sums = pl.pallas_call(
        attention_kernel,
        name="attention",
        out_shape=(shape(ROWS, W), shape(ROWS, W), shape(2 * NSEQ, 2, RLEN, W)),
        in_specs=[SM, VM, VM, VM],
        out_specs=(VM, VM, VM),
        scratch_shapes=[pltpu.VMEM((2 * NSEQ, 2, RLEN, W), F32)],
        compiler_params=pltpu.CompilerParams(vmem_limit_bytes=60 * 1024 * 1024),
    )(read_slot, q, ga, kv.reshape(2, 2 * NSEQ, RLEN, W))
    out, gh, ge = pl.pallas_call(
        scatter_kernel,
        name="project_scatter",
        out_shape=(shape(ROWS, W), shape(ROWS, W), shape(2 * ROWS, W)),
        in_specs=[ANY] * 7 + [SM],
        out_specs=(VM, VM, VM),
        scratch_shapes=[
            pltpu.VMEM((2, SIDE, SIDE, Q, W), BF16), pltpu.VMEM((SIDE, SIDE, EQ, W), BF16),
            pltpu.VMEM((2, 2, 2, Q, W), BF16), pltpu.VMEM((2, 2, EQ, W), BF16),
            pltpu.VMEM((2, 2, SIDE, Q, W), BF16), pltpu.VMEM((2, SIDE, EQ, W), BF16),
            weight, weight, weight, weight_out,
            pltpu.VMEM((ROWS + SPAN, W), BF16), pltpu.VMEM((ROWS + SPAN, W), BF16),
            pltpu.VMEM((2, SIDE, Q, W), BF16), pltpu.VMEM((2, SIDE, Q, W), BF16),
            pltpu.VMEM((NSEQ, 2, 2, RLEN, W), BF16),
            pltpu.VMEM((SIDE, 2, EQ, W), BF16), pltpu.VMEM((SIDE, 2, EQ, W), BF16),
            dma((48,)), dma((48,)), dma((8,)),
        ],
        compiler_params=params(1),
    )(
        att, gq, sums.reshape(NSEQ, 2, 2, RLEN, W), wq, wk, wv, wo, send_rows,
    )
    return out, gh, ge.reshape(encoded.shape)


def solution(mesh):
    placed = (
        P("seq", "tensor"),
        P("seq", None, "tensor"),
        P(None, "tensor"),
        P(None, "tensor"),
        P(None, "tensor"),
        P("tensor", None),
        P("seq", None),
        P("seq", None),
        P("seq", "tensor"),
    )
    return jax.shard_map(
        per_device,
        mesh=mesh,
        in_specs=placed,
        out_specs=(P("seq", "tensor"), P("seq", "tensor"), P("seq", None, "tensor")),
        check_vma=False,
    )
```

time: 490 us -> 219 us (0.45)
  waiting for transfers between devices: 290 us -> 0 us
  Pallas kernels: 0 us -> 210 us
  matrix products: 89.3 us -> 0 us
  local copies, waits for them, and re-layouts: 43.6 us -> 6.55 us
  blocking collectives: 32.7 us -> 0 us
  between operations: 14.4 us -> 0.65 us
  other arithmetic: 10.8 us -> 0 us
  starting transfers between devices: 7.7 us -> 0 us
    pallas_call x0 -> x3, Pallas kernels: none -> 210 us  [the longest x1 128 us: per_device(): pl.pallas_call(gather_kernel, name='gather_project', out_shape=(shape(ROW...]
    all_gather x3 -> x0, waiting for transfers between devices: 163 us -> none  [the longest x1 81 us: per_device(): piece = lax.all_gather(encoded, 'tensor', axis=2, tiled=True)]
    reduce_scatter x3 -> x0, waiting for transfers between devices: 125 us -> none  [the longest x1 88.2 us: per_device(): lax.psum_scatter(partial_enc.astype(jnp.bfloat16), 'tensor', scatter_dime...]
    dot_general x17 -> x0, matrix products: 89.3 us -> none  [the longest x1 11.8 us: per_device(): lax.dot_general(grad_value_rows, w_value, contract, preferred_element_typ...]
    all_to_all x1 -> x0, blocking collectives: 32.7 us -> none  [per_device(): lax.all_to_all(slot_grads, 'seq', split_axis=0, concat_axis=0, tiled=True)]
    slice x12 -> x0, local copies, waits for them, and re-layouts: 18.8 us -> none  [the longest x2 6.32 us: per_device(): read_keys = grad_k[1:].at[spans_here - 1].add(edge_grads[0])]
    gather x3 -> x0, local copies, waits for them, and re-layouts: 7.85 us -> none  [the longest x2 4.27 us: per_device(): outgoing = jnp.stack([keys[safe_rows], values[safe_rows]], 1)]
    reshape x3 -> x0, local copies, waits for them, and re-layouts: 5.6 us -> none  [the longest x1 2.76 us: per_device(): read_keys.reshape(spans_here * NEIGH, read_flat)]
  transfers between devices with their start and end apart: 9 -> 0, of which waited for: 5 -> 0; matrix products, arithmetic and copies ran while one was open for 26% -> 0% of each run, Pallas kernels for 0% -> 0%
where the time goes in v2:
time: 219 us; the launch traced here: 217 us
  Pallas kernels  210 us (96%)
  local copies, waits for them, and re-layouts  6.55 us (3%)
    pallas_call x1, Pallas kernels, per_device(): pl.pallas_call(gather_kernel, name='gather_project', out_shape=(shape(ROW...  128 us
    pallas_call x1, Pallas kernels, per_device(): pl.pallas_call(scatter_kernel, name='project_scatter', out_shape=(shape(R...  66.9 us
    pallas_call x1, Pallas kernels, per_device(): pl.pallas_call(attention_kernel, name='attention', out_shape=(shape(ROWS,...  14.5 us
    unnamed x4, local copies, waits for them, and re-layouts  6.55 us

profile of v2, /device:TPU:0, one launch (start us, length us, event | category | flops | bytes accessed | tf_op | source)
XLA Modules:
  0.0 217.0 jit_solution(1461499198024955426)
XLA Ops:
  0.6 1.3 copy.12.slot_ref
  2.0 128.5 %gather_project.1 = (bf16[576,256]{1,0:T(8,128)(2,1)}, bf16[576,256]{1,0:T(8,128)(2,1)}, bf16[2,8,2,128,256]{4,3,2,1,0:T(8,128)(2,1)}, bf16[4,4096,256]{2,1,0:T(...) custom-call(bf16[1024,256]{1,0:T(8,128)(2,1)} %bitcast.6, ...), custom_call_target="tpu_custom_call" | custom-call | tf_op jit(solution)/shard_map/gather_project/pallas_call | solution.py:679
  130.4 14.5 %attention.1 = (bf16[512,256]{1,0:T(8,128)(2,1)}, bf16[512,256]{1,0:T(8,128)(2,1)}, bf16[16,2,128,256]{3,2,1,0:T(8,128)(2,1)}) custom-call(s32[8,2]{1,0:T(8,128)} %copy.12.slot_ref, bf16[576,256]{1,0:T(8,128)(2,1)} %get-tuple-element.16.q_ref, bf16[576,256]{1,0:T(8,128)(2,1)} %get-tuple-element.17.ga_ref, bf16[2,16,128,256]{3,2,1,0:T(8,128)(2,1)} %bitcast.5), custom_call_target="tpu_custom_call" | custom-call | tf_op jit(solution)/shard_map/attention/pallas_call | solution.py:702
  144.9 66.9 %project_scatter.1 = (bf16[512,256]{1,0:T(8,128)(2,1)}, bf16[512,256]{1,0:T(8,128)(2,1)}, bf16[1024,256]{1,0:T(8,128)(2,1)}) custom-call(bf16[512,256]{1,0:T(8,128)(2,1)} %get-tuple-element.19.att_ref, bf16[512,256]{1,0:T(8,128)(2,1)} %get-tuple-element.20.gq_ref, bf16[8,2,2,128,256]{4,3,2,1,0:T(8,128)(2,1)} %bitcast.4, ...), custom_call_target="tpu_custom_call" | custom-call | tf_op jit(solution)/shard_map/project_scatter/pallas_call | solution.py:711
  211.8 1.7 copy.16
  213.4 1.7 copy.17
  215.1 1.9 copy.18

commit v3 on v0

v3 whole, which is shorter than its diff:
```python
import functools

import jax
import jax.numpy as jnp
from jax import lax
from jax.experimental import pallas as pl
from jax.experimental.pallas import tpu as pltpu
from jax.sharding import PartitionSpec as P

SPAN = 64
NEIGH = 2
RLEN = 128
HEAD_DIM = 128
NSEQ = 8
SIDE = 4
NT = SIDE * SIDE
W = 256
ROWS = 512
Q = ROWS // SIDE
EQ = 2 * ROWS // SIDE
MESH = pl.DeviceIdType.MESH
ANY = pl.BlockSpec(memory_space=pl.ANY)
VM = pl.BlockSpec(memory_space=pltpu.VMEM)
SM = pl.BlockSpec(memory_space=pltpu.SMEM)
F32 = jnp.float32
BF16 = jnp.bfloat16
NT_DIMS = (((1,), (1,)), ((), ()))
TN_DIMS = (((0,), (0,)), ((), ()))
SPANS = ROWS // SPAN
SLOTS = 2 * NSEQ
HEADS = W // HEAD_DIM
HALF = RLEN // 2
NONE = SPANS * NEIGH
OFFSETS = (0, 3, 1, 2)
SHARES = {"K": (256,), "V": (256,), "Q": (), "O": (256,)}
ALONE = 256
UNROLL = 2


ORDER = (
    0, 46, 92, 149, 195, 211, 227, 199, 200, 197, 198, 175, 115, 196, 167, 174, 136, 168, 100, 150, 32, 78,
    48, 47, 79, 72, 291, 207, 65, 85, 33, 204, 71, 205, 206, 119, 203, 155, 177, 36, 34, 202, 154, 76, 83,
    140, 176, 201, 74, 81, 80, 152, 49, 151, 94, 50, 51, 54, 53, 1, 64, 86, 232, 52, 178, 171, 179, 82, 172,
    104, 160, 169, 114, 58, 57, 180, 188, 19, 84, 231, 215, 55, 56, 216, 2, 143, 89, 87, 18, 69, 67, 37, 35,
    26, 62, 210, 164, 135, 208, 73, 209, 156, 153, 157, 122, 129, 60, 128, 98, 75, 61, 88, 59, 3, 66, 25, 5,
    6, 90, 239, 68, 223, 40, 39, 161, 63, 38, 93, 101, 190, 121, 11, 159, 158, 192, 77, 118, 147, 165, 21, 4,
    7, 8, 23, 28, 91, 30, 163, 142, 170, 117, 70, 139, 107, 137, 261, 22, 20, 126, 258, 263, 264, 42, 133, 15,
    214, 12, 259, 27, 131, 124, 108, 213, 10, 243, 41, 262, 9, 260, 29, 162, 182, 96, 103, 24, 105, 44, 43,
    132, 173, 244, 245, 16, 181, 116, 212, 97, 102, 14, 13, 95, 31, 45, 166, 246, 247, 221, 189, 222, 265,
    270, 267, 268, 269, 272, 17, 271, 266, 138, 228, 219, 220, 130, 145, 109, 123, 226, 229, 146, 125, 248,
    111, 249, 225, 120, 144, 218, 217, 230, 106, 99, 112, 110, 250, 224, 255, 184, 186, 251, 141, 256, 235,
    236, 253, 252, 257, 254, 233, 234, 134, 276, 127, 277, 274, 275, 273, 183, 185, 191, 193, 148, 238, 237,
    241, 113, 240, 278, 279, 242, 187, 194, 280, 283, 287, 285, 282, 284, 286, 281, 293, 288, 292, 324, 289,
    325, 327, 329, 326, 290, 294, 306, 328, 308, 302, 295, 305, 309, 348, 333, 331, 338, 332, 342, 317, 330,
    349, 353, 334, 350, 352, 335, 319, 316, 310, 351, 303, 313, 298, 323, 301, 320, 321, 318, 307, 304, 314,
    296, 322, 355, 362, 354, 359, 358, 356, 366, 357, 337, 341, 336, 339, 311, 300, 360, 363, 361, 365, 343,
    297, 315, 312, 340, 397, 400, 401, 399, 398, 347, 346, 345, 344, 299, 364, 367, 368, 372, 370, 369, 371,
    373, 376, 377, 375, 374, 402, 407, 406, 404, 414, 403, 410, 405, 378, 383, 409, 413, 382, 380, 408, 411,
    381, 379, 386, 390, 384, 387, 385, 389, 415, 412, 416, 418, 420, 417, 419, 388, 391, 392, 395, 396, 393,
    394,
)
MESSAGES = 342


def wrap(value, count):
    return lax.rem(value + count, count)


class Grid:
    def __init__(self):
        self.seq = lax.axis_index("seq")
        tensor = lax.axis_index("tensor")
        self.z = lax.div(tensor, SIDE)
        self.x = lax.rem(tensor, SIDE)
        self.y = lax.div(self.seq, 2)
        self.core = lax.rem(self.seq, 2)

    def at(self, axis):
        return self.z if axis == "z" else self.x

    def along(self, axis, step):
        if axis == "z":
            return {"tensor": wrap(self.z + step, SIDE) * SIDE + self.x}
        if axis == "x":
            return {"tensor": self.z * SIDE + wrap(self.x + step, SIDE)}
        if axis == "y":
            return {"seq": wrap(self.y + step, SIDE) * 2 + self.core}
        if axis == "core":
            return {"seq": self.y * 2 + (1 - self.core)}
        return {"seq": wrap(self.seq + step, NSEQ)}

    def barrier(self):
        sem = pltpu.get_barrier_semaphore()
        peers = [self.along(axis, k) for axis in "zx" for k in range(1, SIDE)]
        peers += [self.along("seq", k) for k in range(1, NSEQ)]
        for peer in peers:
            pl.semaphore_signal(sem, inc=1, device_id=peer, device_id_type=MESH)
        pl.semaphore_wait(sem, len(peers))


class Plan:
    def __init__(self, send, recv, local):
        self.send, self.recv, self.local = send, recv, local
        self.actions, self.copies, self.landed, self.left = {}, {}, set(), set()
        self.messages = self.locals = 0

    def message(self, name, src, dst, peer, land, after=()):
        self.actions[name] = ("message", (src, dst, peer, land, self.messages), after, ())
        self.messages += 1

    def step(self, name, work, after=(), sent=()):
        self.actions[name] = ("step", work, after, sent)

    def load(self, name, src, dst):
        self.actions[name] = ("load", (src, dst, self.locals), (), ())
        self.locals += 1

    def need(self, name):
        if name in self.landed:
            return
        kind, data, _, _ = self.actions[name]
        assert name in self.copies, name
        if kind == "message":
            land = data[3]
            pltpu.make_async_copy(land, land, self.recv.at[data[4]]).wait()
        else:
            self.copies[name].wait()
        self.landed.add(name)

    def leave(self, name):
        if name not in self.left:
            self.copies[name].wait_send()
            self.left.add(name)

    def run(self, name):
        kind, data, after, sent = self.actions[name]
        for other in after:
            self.need(other)
        for other in sent:
            self.leave(other)
        if kind == "message":
            src, dst, peer, _, number = data
            copy = pltpu.make_async_remote_copy(
                src_ref=src,
                dst_ref=dst,
                send_sem=self.send.at[number],
                recv_sem=self.recv.at[number],
                device_id=peer,
                device_id_type=MESH,
            )
            copy.start()
            self.copies[name] = copy
        elif kind == "load":
            src, dst, number = data
            copy = pltpu.make_async_copy(src, dst, self.local.at[number])
            copy.start()
            self.copies[name] = copy
        else:
            data()
            self.landed.add(name)

    def finish(self):
        for name, (kind, _, _, _) in self.actions.items():
            if kind != "step":
                self.need(name)
            if kind == "message":
                self.leave(name)


def signs():
    return (("+", 1), ("-", -1))


def add_gather(plan, g, n, cut, ring, own, buf):
    rows = buf.shape[2]
    i, j = g.at(cut), g.at(ring)

    def slot(dj, di):
        return buf.at[wrap(j + dj, SIDE), wrap(i + di, SIDE)]

    def quarter(di):
        return own.at[pl.ds(pl.multiple_of(wrap(i + di, SIDE) * rows, rows), rows)]

    plan.load((n, "l"), quarter(0), slot(0, 0))
    for k in (1, 3, 2):
        plan.message((n, "x", k), quarter(k), slot(0, 0), g.along(cut, k), slot(0, SIDE - k))
    for d in OFFSETS:
        src, after = (slot(0, d), ((n, "x", SIDE - d),)) if d else (quarter(0), ())
        for sign, step in signs():
            plan.message(
                (n, "s", d, sign), src, slot(0, d), g.along(ring, step), slot(-step + SIDE, d), after
            )
    for d in OFFSETS:
        sign, step = ("+", 1) if d in (0, 1) else ("-", -1)
        block = slot(SIDE - step, d)
        plan.message((n, "f", d), block, block, g.along(ring, step), slot(2, d), ((n, "s", d, sign),))
    names = [(n, "l")] + [(n, "x", k) for k in (1, 2, 3)] + [(n, "f", d) for d in OFFSETS]
    return names + [(n, "s", d, sign) for d in OFFSETS for sign in "+-"]


def add_weight(plan, g, n, cut, own, full, wide):
    i = g.at(cut)
    needs = {e: [] for e in OFFSETS}
    plan.load((n, "l"), own, full.at[i])
    needs[0].append((n, "l"))

    def cutout(ref, start, size):
        rows = pl.ds(pl.multiple_of(start, 128), size)
        return ref.at[:, rows] if wide else ref.at[rows]

    def add_piece(p, begin, size, shared):
        half = SIDE * size if shared else size
        other = begin + (1 - g.core) * half
        region = begin + g.core * half

        def chunk(dy):
            return region + wrap(g.y + dy, SIDE) * size if shared else region

        def at(e, start, length=size):
            return cutout(full.at[wrap(i + e, SIDE)], start, length)

        def ends(sign):
            return 0 if sign == "+" else size // 2

        here = chunk(0)
        for sign, step in signs():
            plan.message(
                (p, "n", sign), cutout(own, here, size), at(0, here), g.along(cut, step),
                at(SIDE - step, here),
            )
        for sign, step in signs():
            part = at(SIDE - step, here + ends(sign), size // 2)
            plan.message(
                (p, "h", sign), part, part, g.along(cut, step), at(2, here + ends(sign), size // 2),
                ((p, "n", sign),),
            )
        have = {3: [(p, "n", "+")], 1: [(p, "n", "-")], 2: [(p, "h", "+"), (p, "h", "-")]}
        if shared:
            for e in (3, 1, 2):
                for sign, step in signs():
                    plan.message(
                        (p, "y", e, sign), at(e, here), at(e, here), g.along("y", step),
                        at(e, chunk(SIDE - step)), tuple(have[e]),
                    )
            for e, sign, step, length in ((3, "+", 1, size), (1, "-", -1, size), (2, "+", 1, size // 2), (2, "-", -1, size // 2)):
                off = ends(sign) if e == 2 else 0
                part = at(e, chunk(SIDE - step) + off, length)
                plan.message(
                    (p, "z", e, sign), part, part, g.along("y", step), at(e, chunk(2) + off, length),
                    ((p, "y", e, sign),),
                )
            for e, last in ((3, "+"), (1, "-"), (2, "+-")):
                have[e] += [(p, "y", e, "+"), (p, "y", e, "-")] + [(p, "z", e, sign) for sign in last]
        for e in (3, 1, 2):
            block = at(e, region, half)
            plan.message(
                (p, "c", e), block, block, g.along("core", 1), at(e, other, half), tuple(have[e])
            )
            needs[e] += have[e] + [(p, "c", e)]

    begin = 0
    for count, size in enumerate(SHARES[n]):
        add_piece((n, count), begin, size, True)
        begin += 2 * SIDE * size
    while begin < NT * W:
        add_piece((n, begin // (2 * ALONE) + 8), begin, ALONE, False)
        begin += 2 * ALONE
    return needs


def lanes(blocks):
    return jnp.concatenate(blocks, 1)


def add_project(plan, g, n, cut, ring, buf, have, full, needs, wide, dst, sender):
    i = g.at(cut)

    def columns(e):
        at = wrap(i + e, SIDE)
        total = None
        for m in range(SIDE):
            if ring == "z":
                left = lanes([buf[m, k] for k in range(SIDE)])
            else:
                left = lanes([buf[k, m] for k in range(SIDE)])
            depth = pl.ds(m * SIDE * W, SIDE * W)
            if wide:
                term = lax.dot_general(left, full[at, :, depth], NT_DIMS, preferred_element_type=F32)
            else:
                term = jnp.dot(left, full[at, depth, :], preferred_element_type=F32)
            total = term if total is None else total + term
        return total.astype(BF16)

    def make(e):
        def work():
            if e:
                sender[e] = columns(e).reshape(sender.shape[1:])
            else:
                dst(i)[...] = columns(e).reshape(sender.shape[1:])

        return work

    for e in OFFSETS:
        plan.step((n, "p", e), make(e), tuple(have + needs[e]))
        if e:
            plan.message(
                (n, "o", e), sender.at[e], dst(i), g.along(cut, e), dst(wrap(i - e, SIDE)),
                ((n, "p", e),),
            )
    return [(n, "p", 0)] + [(n, "o", e) for e in (1, 2, 3)]


def add_scatter(plan, g, n, cut, ring, own, own_step, got, parts, one, two, make, out, old=(), final=None):
    i, j = g.at(cut), g.at(ring)

    def keep():
        got[i] = own[i]

    plan.step((n, "k"), keep, (own_step,))
    for k in (1, 3, 2):
        peer = wrap(i + k, SIDE)
        plan.message(
            (n, "x", k), own.at[peer], got.at[i], g.along(cut, k), got.at[wrap(i - k, SIDE)],
            (own_step,),
        )
    swapped = ((n, "k"), (n, "x", 1), (n, "x", 2), (n, "x", 3))

    def part(dj, where=None):
        block = parts.at[wrap(j + dj, SIDE)]
        return block if where is None else block.at[pl.ds(2 * where, 2)]

    def fill(dj):
        def work():
            row = wrap(j + dj, SIDE)

            @pl.loop(0, SIDE)
            def _(k):
                t = row * SIDE + k if ring == "z" else k * SIDE + row
                parts[row, k] = make(t).astype(BF16)

        return work

    def add(ref, *others):
        total = ref[...].astype(F32)
        for other in others:
            total = total + other[...].astype(F32)
        ref[...] = total.astype(BF16)

    for dj in (2, 1, 3, 0):
        plan.step((n, "f", dj), fill(dj), swapped, old)
    plan.message((n, "n", 0), part(2, 0), one.at[0], g.along(ring, -1), one.at[0], ((n, "f", 2),))
    plan.message((n, "n", 1), part(2, 1), one.at[1], g.along(ring, 1), one.at[1], ((n, "f", 2),))
    plan.step((n, "r", 0), lambda: add(part(3, 0), one.at[0]), ((n, "f", 3), (n, "n", 0)))
    plan.step((n, "r", 1), lambda: add(part(1, 1), one.at[1]), ((n, "f", 1), (n, "n", 1)))
    for where in range(2):
        half = pl.ds(2 * where, 2)
        up, down = two.at[0, half], two.at[1, half]
        plan.message(
            (n, "u", where), part(1, where), up, g.along(ring, 1), up, ((n, "r", 1) if where else (n, "f", 1),)
        )
        plan.message(
            (n, "d", where), part(3, where), down, g.along(ring, -1), down, ((n, "f", 3) if where else (n, "r", 0),)
        )
        plan.step(
            (n, "t", where),
            functools.partial(add, part(0, where), up, down),
            ((n, "f", 0), (n, "u", where), (n, "d", where)),
        )
    totals = ((n, "t", 0), (n, "t", 1))
    ready = parts.at[j]
    if final is not None:
        ready = final

        def turn():
            for k in range(SIDE):
                final[k] = parts[j, k].astype(F32).T.astype(BF16).reshape(final.shape[1:])

        plan.step((n, "v"), turn, totals)
        totals = ((n, "v"),)
    for k in (1, 3, 2):
        plan.message(
            (n, "b", k), ready.at[wrap(i + k, SIDE)], out(i), g.along(cut, k),
            out(wrap(i - k, SIDE)), totals,
        )

    def own_rows():
        out(i)[...] = ready[i]

    plan.step((n, "b", 0), own_rows, totals)


def register(
    plan, g,
    enc_ref, hid_ref, gout_ref, wq_ref, wk_ref, wv_ref, wo_ref, rows_ref, slot_ref,
    out_ref, gh_ref, ge_ref,
    enc_all, hid_all, gout_all, wq, wk, wv, wo, kv_send, q_send, ga_send, own_k, own_v, stage_k, stage_v,
    k_in, v_in, q_ext, ga_ext, q_span, ga_span, probs, att, gq, tok_a, tok_c, got_a, got_c, reads,
    slot_out, slot_in, gkv, gkv_t, gkv_got, parts_c, parts_enc, one_a, two_a, one_c, two_c, one_enc, two_enc,
    final_c, final_enc, chain,
):
    scale = HEAD_DIM ** (-0.5)
    all_weights = {}
    for n, cut, own, full in (("K", "x", wk_ref, wk), ("V", "x", wv_ref, wv), ("Q", "z", wq_ref, wq), ("O", "z", wo_ref, wo)):
        all_weights[n] = add_weight(plan, g, n, cut, own, full, n == "O")
    enc = add_gather(plan, g, "E", "x", "z", enc_ref, enc_all)
    hid = add_gather(plan, g, "H", "z", "x", hid_ref, hid_all)
    gout = add_gather(plan, g, "G", "z", "x", gout_ref, gout_all)

    per = EQ // RLEN
    for n, full, own, stage, sender, land in (
        ("K", wk, own_k, stage_k, kv_send.at[0], k_in), ("V", wv, own_v, stage_v, kv_send.at[1], v_in)
    ):
        def rows(i, own=own):
            return own.at[pl.ds(i * per, per)]

        made = add_project(
            plan, g, n, "x", "z", enc_all, enc, full, all_weights[n], False, rows, sender
        )

        def pick(own=own, stage=stage, land=land):
            @pl.loop(0, NSEQ)
            def _(r):
                for s in range(2):
                    stage[r, s] = own[jnp.maximum(rows_ref[0, 2 * r + s], 0)]

            land[g.seq] = stage[g.seq]

        plan.step((n, "x"), pick, tuple(made))
        for k in range(1, NSEQ):
            plan.message(
                (n, "a", k), stage.at[wrap(g.seq + k, NSEQ)], land.at[g.seq], g.along("seq", k),
                land.at[wrap(g.seq - k, NSEQ)], ((n, "x"),),
            )

    head, tail = pl.ds(0, SPAN), pl.ds(ROWS, SPAN)
    row = col = None

    def shift_rows(by, limit=None):
        row = lax.broadcasted_iota(jnp.int32, (Q, Q + SPAN), 0)
        col = lax.broadcasted_iota(jnp.int32, (Q, Q + SPAN), 1)
        picked = col == row + by
        if limit is not None:
            picked = jnp.logical_and(picked, col < limit)
        return picked.astype(BF16)

    for n, buf, have, full, ext, span, sender in (
        ("Q", hid_all, hid, wq, q_ext, q_span, q_send), ("O", gout_all, gout, wo, ga_ext, ga_span, ga_send)
    ):
        def rows(i, ext=ext):
            return ext.at[pl.ds(pl.multiple_of(i * Q, Q), Q)]

        made = add_project(
            plan, g, n, "z", "x", buf, have, full, all_weights[n], n == "O", rows, sender
        )
        plan.message(
            (n, "e"), ext.at[head], ext.at[tail], g.along("seq", NSEQ - 1), ext.at[tail], tuple(made)
        )

        def align(ext=ext, span=span):
            for m in range(SIDE):
                limit = None
                if m == SIDE - 1:
                    limit = jnp.where(g.seq == NSEQ - 1, Q, Q + SPAN)
                moved = jnp.dot(
                    shift_rows(SPAN - 1, limit), ext[m * Q : (m + 1) * Q + SPAN, :],
                    preferred_element_type=F32,
                )
                span[m * Q : (m + 1) * Q, :] = moved.astype(BF16)

        plan.step((n, "t"), align, tuple(made) + ((n, "e"),))

    def tables():
        for kind in range(2):
            reads[kind, NONE] = jnp.zeros((RLEN, HEAD_DIM), F32)
        ids = [slot_ref[p // NEIGH, p % NEIGH] for p in range(NONE)]
        targets = [rows_ref[0, j] for j in range(NONE)]
        for line, values in ((0, ids), (2, targets)):
            for p in range(NONE):
                before, latest = jnp.int32(NONE), jnp.int32(NONE)
                for q in range(NONE):
                    if q < p:
                        before = jnp.where(values[q] == values[p], q, before)
                    latest = jnp.where(values[q] == p, q, latest)
                chain[line, p] = before
                chain[line + 1, p] = latest

    plan.step(("T", "t"), tables)

    def read(ref, u, cols):
        picked = []
        for j in range(NEIGH):
            s = slot_ref[u, j]
            picked.append(ref[lax.div(s, 2), lax.rem(s, 2), :, cols])
        return jnp.concatenate(picked, 0)

    def forward(h):
        cols = slice(h * HEAD_DIM, (h + 1) * HEAD_DIM)

        def work():
            @pl.loop(0, SPANS, unroll=UNROLL)
            def _(u):
                here = pl.ds(pl.multiple_of(u * SPAN, SPAN), SPAN)
                k, v = read(k_in, u, cols), read(v_in, u, cols)
                scores = lax.dot_general(
                    q_span[here, cols], k, NT_DIMS, preferred_element_type=F32
                ) * scale
                peak = jnp.max(scores, axis=-1, keepdims=True)
                weights = jnp.exp(scores - peak)
                prob = weights / jnp.sum(weights, axis=-1, keepdims=True)
                probs[h, u] = prob
                context = jnp.dot(prob.astype(BF16), v, preferred_element_type=F32)
                att[pl.ds(pl.multiple_of(u * SPAN, SPAN) + SPAN, SPAN), cols] = context.astype(BF16)

        return work

    def backward(h):
        cols = slice(h * HEAD_DIM, (h + 1) * HEAD_DIM)

        def work():
            @pl.loop(0, SPANS, unroll=UNROLL)
            def _(u):
                here = pl.ds(pl.multiple_of(u * SPAN, SPAN), SPAN)
                k, v = read(k_in, u, cols), read(v_in, u, cols)
                prob = probs[h, u]
                q, gr = q_span[here, cols], ga_span[here, cols]
                grad_probs = lax.dot_general(gr, v, NT_DIMS, preferred_element_type=F32)
                dot_sum = jnp.sum(grad_probs * prob, axis=-1, keepdims=True)
                grad_scores = (prob * (grad_probs - dot_sum) * scale).astype(BF16)
                grad_q = jnp.dot(grad_scores, k, preferred_element_type=F32)
                gq[pl.ds(pl.multiple_of(u * SPAN, SPAN) + SPAN, SPAN), cols] = grad_q.astype(BF16)
                grad_k = lax.dot_general(grad_scores, q, TN_DIMS, preferred_element_type=F32)
                grad_v = lax.dot_general(
                    prob.astype(BF16), gr, TN_DIMS, preferred_element_type=F32
                )
                for j in range(NEIGH):
                    part = slice(j * RLEN, (j + 1) * RLEN)
                    p = NEIGH * u + j
                    before = chain[0, p]
                    reads[0, p] = grad_k[part] + reads[0, before]
                    reads[1, p] = grad_v[part] + reads[1, before]

            @pl.loop(0, SLOTS)
            def _(s):
                latest = chain[1, s]
                for r in range(2):
                    for kind in range(2):
                        slot_out[h, r, lax.div(s, 2), lax.rem(s, 2), kind] = reads[
                            kind, latest, r * HALF : (r + 1) * HALF, :
                        ].astype(BF16)

            for r in range(2):
                slot_in[h, r, g.seq] = slot_out[h, r, g.seq]

        return work

    landed = tuple((n, "a", k) for n in "KV" for k in range(1, NSEQ)) + (("K", "x"), ("V", "x"))
    for h in range(HEADS):
        plan.step(("F", h), forward(h), landed + (("Q", "t"),))
    for h in range(HEADS):
        plan.step(("B", h), backward(h), (("F", h), ("O", "t"), ("T", "t")))
        for r in range(2):
            for k in range(1, NSEQ):
                plan.message(
                    ("S", h, r, "a", k), slot_out.at[h, r, wrap(g.seq + k, NSEQ)], slot_in.at[h, r, g.seq],
                    g.along("seq", k), slot_in.at[h, r, wrap(g.seq - k, NSEQ)], (("B", h),),
                )

    last = pl.ds(ROWS, SPAN)

    def out_part(t):
        depth = pl.ds(pl.multiple_of(t * W, W), W)
        return sum(
            jnp.dot(got_a[k], wo[k, :, depth], preferred_element_type=F32) for k in range(SIDE)
        )

    def hidden_part(t):
        depth = pl.ds(pl.multiple_of(t * W, W), W)
        return sum(
            jnp.dot(wq[k, depth, :], got_c[k], preferred_element_type=F32)
            for k in range(SIDE)
        )

    gone = [("H", "f", d) for d in OFFSETS]
    gone += [("H", "s", d, sign) for d in (1, 2, 3) for sign in "+-"]
    for n, src, made, make, tok, got, parts, one, two, result, old, final in (
        ("A", att, (("F", 0), ("F", 1)), out_part, tok_a, got_a, hid_all, one_a, two_a, out_ref, tuple(gone), None),
        ("C", gq, (("B", 0), ("B", 1)), hidden_part, tok_c, got_c, parts_c, one_c, two_c, gh_ref, (), final_c),
    ):
        plan.message((n, "e"), src.at[last], src.at[head], g.along("seq", 1), src.at[head], made)

        def align(src=src, tok=tok, final=final):
            @pl.when(g.seq == 0)
            def _():
                src[head, :] = jnp.zeros((SPAN, W), BF16)

            for m in range(SIDE):
                moved = jnp.dot(
                    shift_rows(1), src[m * Q : (m + 1) * Q + SPAN, :], preferred_element_type=F32
                )
                tok[m] = (moved if final is None else moved.T).astype(BF16)

        plan.step((n, "t"), align, made + ((n, "e"),))

        def rows(i, result=result):
            return result.at[pl.ds(pl.multiple_of(i * Q, Q), Q)]

        add_scatter(
            plan, g, n, "z", "x", tok, (n, "t"), got, parts, one, two, make, rows, old, final
        )

    def owner_sums(r):
        def work():
            @pl.loop(0, NSEQ)
            def _(o):
                for slot in range(2):
                    p = 2 * o + slot
                    before = chain[2, p]
                    for kind in range(2):
                        for h in range(HEADS):
                            rows = slice(h * HALF, (h + 1) * HALF)
                            value = slot_in[h, r, o, slot, kind].astype(F32)
                            reads[kind, p, rows, :] = value + reads[kind, before, rows, :]

            for n in range(NSEQ):
                latest = chain[3, n]
                for kind in range(2):
                    for h in range(HEADS):
                        rows = slice(h * HALF, (h + 1) * HALF)
                        cols = slice(h * HEAD_DIM, (h + 1) * HEAD_DIM)
                        place = slice((n % per) * HALF, (n % per + 1) * HALF)
                        gkv[n // per, kind, place, cols] = reads[kind, latest, rows, :].astype(BF16)
            for k in range(SIDE):
                for kind in range(2):
                    gkv_t[r, k, kind] = gkv[k, kind].astype(F32).T.astype(BF16)

        return work

    def enc_part(r):
        def make(t):
            depth = pl.ds(pl.multiple_of(t * W, W), W)
            total = None
            for kind, w in ((0, wk), (1, wv)):
                for k in range(SIDE):
                    term = jnp.dot(
                        w[k, depth, :], gkv_got[r, k, kind], preferred_element_type=F32
                    )
                    total = term if total is None else total + term
            return total

        return make

    for r in range(2):
        came = tuple(("S", h, r, "a", k) for h in range(HEADS) for k in range(1, NSEQ))
        plan.step(("W", r), owner_sums(r), came + (("B", 0), ("B", 1)))

        def rows(i, r=r):
            return ge_ref.at[pl.ds(i * per, per), pl.ds(r * HALF, HALF)]

        add_scatter(
            plan, g, ("Y", r), "x", "z", gkv_t.at[r], ("W", r), gkv_got.at[r], parts_enc.at[r],
            one_enc.at[r], two_enc.at[r], enc_part(r), rows, (), final_enc.at[r],
        )


def kernel(*refs):
    *refs, send, recv, local = refs
    g = Grid()
    plan = Plan(send, recv, local)
    register(plan, g, *refs)
    names = list(plan.actions)
    assert sorted(ORDER) == list(range(len(names)))
    g.barrier()
    for number in ORDER:
        plan.run(names[number])
    plan.finish()


def scratch():
    def vmem(*dims, dtype=BF16):
        return pltpu.VMEM(dims, dtype)

    weight = vmem(SIDE, NT * W, W)
    quarters = vmem(SIDE, Q, W)
    return [
        vmem(SIDE, SIDE, EQ, W), vmem(SIDE, SIDE, Q, W), vmem(SIDE, SIDE, Q, W),
        weight, weight, weight, vmem(SIDE, W, NT * W),
        vmem(2, SIDE, EQ // RLEN, RLEN, W), quarters, quarters,
        vmem(NSEQ, RLEN, W), vmem(NSEQ, RLEN, W),
        vmem(NSEQ, 2, RLEN, W), vmem(NSEQ, 2, RLEN, W), vmem(NSEQ, 2, RLEN, W), vmem(NSEQ, 2, RLEN, W),
        vmem(ROWS + SPAN, W), vmem(ROWS + SPAN, W), vmem(ROWS, W), vmem(ROWS, W),
        vmem(HEADS, SPANS, SPAN, NEIGH * RLEN, dtype=F32),
        vmem(ROWS + SPAN, W), vmem(ROWS + SPAN, W),
        quarters, vmem(SIDE, W, Q), quarters, vmem(SIDE, W, Q),
        vmem(2, NONE + 1, RLEN, HEAD_DIM, dtype=F32),
        vmem(HEADS, 2, NSEQ, 2, 2, HALF, HEAD_DIM), vmem(HEADS, 2, NSEQ, 2, 2, HALF, HEAD_DIM),
        vmem(SIDE, 2, Q, W), vmem(2, SIDE, 2, W, Q), vmem(2, SIDE, 2, W, Q),
        vmem(SIDE, SIDE, W, Q), vmem(2, SIDE, SIDE, W, Q),
        vmem(2, 2, Q, W), vmem(2, SIDE, Q, W), vmem(2, 2, W, Q), vmem(2, SIDE, W, Q),
        vmem(2, 2, 2, W, Q), vmem(2, 2, SIDE, W, Q),
        quarters, vmem(2, SIDE, 2, HALF, W), pltpu.SMEM((4, NONE), jnp.int32),
    ]


def shape(*dims, dtype=BF16):
    return jax.ShapeDtypeStruct(dims, dtype)


def per_device(hidden, encoded, w_query, w_key, w_value, w_out, send_rows, read_slot, grad_out):
    dma = pltpu.SemaphoreType.DMA
    out, gh, ge = pl.pallas_call(
        kernel,
        name="cross_attention",
        out_shape=(shape(ROWS, W), shape(ROWS, W), shape(NSEQ, RLEN, W)),
        in_specs=[ANY] * 7 + [SM, SM],
        out_specs=(VM, VM, VM),
        scratch_shapes=scratch() + [dma((MESSAGES,)), dma((MESSAGES,)), dma((7,))],
        compiler_params=pltpu.CompilerParams(
            collective_id=0, has_side_effects=True, vmem_limit_bytes=63 * 1024 * 1024
        ),
    )(
        encoded.reshape(2 * ROWS, W), hidden, grad_out, w_query, w_key, w_value, w_out, send_rows, read_slot,
    )
    return out, gh, ge


def solution(mesh):
    placed = (
        P("seq", "tensor"),
        P("seq", None, "tensor"),
        P(None, "tensor"),
        P(None, "tensor"),
        P(None, "tensor"),
        P("tensor", None),
        P("seq", None),
        P("seq", None),
        P("seq", "tensor"),
    )
    return jax.shard_map(
        per_device,
        mesh=mesh,
        in_specs=placed,
        out_specs=(P("seq", "tensor"), P("seq", "tensor"), P("seq", None, "tensor")),
        check_vma=False,
    )
```

time: 490 us -> 187 us (0.38)
  waiting for transfers between devices: 290 us -> 0 us
  Pallas kernels: 0 us -> 179 us
  matrix products: 89.3 us -> 0 us
  local copies, waits for them, and re-layouts: 43.6 us -> 6.55 us
  blocking collectives: 32.7 us -> 0 us
  between operations: 14.4 us -> 0.64 us
  other arithmetic: 10.8 us -> 0 us
  starting transfers between devices: 7.7 us -> 0 us
    pallas_call x0 -> x1, Pallas kernels: none -> 179 us  [per_device(): pl.pallas_call(kernel, name='cross_attention', out_shape=(shape(ROWS, W),...]
    all_gather x3 -> x0, waiting for transfers between devices: 163 us -> none  [the longest x1 81 us: per_device(): piece = lax.all_gather(encoded, 'tensor', axis=2, tiled=True)]
    reduce_scatter x3 -> x0, waiting for transfers between devices: 125 us -> none  [the longest x1 88.2 us: per_device(): lax.psum_scatter(partial_enc.astype(jnp.bfloat16), 'tensor', scatter_dime...]
    dot_general x17 -> x0, matrix products: 89.3 us -> none  [the longest x1 11.8 us: per_device(): lax.dot_general(grad_value_rows, w_value, contract, preferred_element_typ...]
    all_to_all x1 -> x0, blocking collectives: 32.7 us -> none  [per_device(): lax.all_to_all(slot_grads, 'seq', split_axis=0, concat_axis=0, tiled=True)]
    slice x12 -> x0, local copies, waits for them, and re-layouts: 18.8 us -> none  [the longest x2 6.32 us: per_device(): read_keys = grad_k[1:].at[spans_here - 1].add(edge_grads[0])]
    gather x3 -> x0, local copies, waits for them, and re-layouts: 7.85 us -> none  [the longest x2 4.27 us: per_device(): outgoing = jnp.stack([keys[safe_rows], values[safe_rows]], 1)]
    reshape x3 -> x0, local copies, waits for them, and re-layouts: 5.6 us -> none  [the longest x1 2.76 us: per_device(): read_keys.reshape(spans_here * NEIGH, read_flat)]
  transfers between devices with their start and end apart: 9 -> 0, of which waited for: 5 -> 0; matrix products, arithmetic and copies ran while one was open for 26% -> 0% of each run, Pallas kernels for 0% -> 0%
where the time goes in v3:
time: 187 us; the launch traced here: 186 us
  Pallas kernels  179 us (96%)
  local copies, waits for them, and re-layouts  6.55 us (4%)
    pallas_call x1, Pallas kernels, per_device(): pl.pallas_call(kernel, name='cross_attention', out_shape=(shape(ROWS, W),...  179 us
    unnamed x4, local copies, waits for them, and re-layouts  6.55 us

profile of v3, /device:TPU:0, one launch (start us, length us, event | category | flops | bytes accessed | tf_op | source)
XLA Modules:
  0.0 185.9 jit_solution(10583894672193203476)
XLA Ops:
  0.6 1.3 copy.12.refs_8_
  2.0 178.7 %cross_attention.1 = (bf16[512,256]{1,0:T(8,128)(2,1)}, bf16[512,256]{1,0:T(8,128)(2,1)}, bf16[8,128,256]{2,1,0:T(8,128)(2,1)}) custom-call(bf16[1024,256]{1,0:T(8,128)(2,1)} %bitcast.1, bf16[512,256]{1,0:T(8,128)(2,1)} %refs_1_.1, bf16[512,256]{1,0:T(8,128)(2,1)} %refs_2_.1, bf16[4096,256]{1,0:T(8,128)(2,1)} %refs_3_.1, bf16[4096,256]{1,0:T(8,128)(2,1)} %refs_4_.1, ...), custom_call_target="tpu_custom_call" | custom-call | tf_op jit(solution)/shard_map/cross_attention/pallas_call | solution.py:710
  180.7 1.7 copy.16
  182.4 1.7 copy.17
  184.1 1.9 %copy.18 = bf16[8,128,256]{2,1,0:T(8,128)(2,1)} copy(bf16[8,128,256]{2,1,0:T(8,128)(2,1)} %get-tuple-element.8) | data formatting | bytes 1048576

commit v4 on v3

--- a/solution.py
+++ b/solution.py
@@ -33,33 +33,38 @@
 NONE = SPANS * NEIGH
 OFFSETS = (0, 3, 1, 2)
 SHARES = {"K": (256,), "V": (256,), "Q": (), "O": (256,)}
-ALONE = 256
+ALONE = 512
 UNROLL = 2
 
 
 ORDER = (
-    0, 46, 92, 149, 195, 211, 227, 199, 200, 197, 198, 175, 115, 196, 167, 174, 136, 168, 100, 150, 32, 78,
-    48, 47, 79, 72, 291, 207, 65, 85, 33, 204, 71, 205, 206, 119, 203, 155, 177, 36, 34, 202, 154, 76, 83,
-    140, 176, 201, 74, 81, 80, 152, 49, 151, 94, 50, 51, 54, 53, 1, 64, 86, 232, 52, 178, 171, 179, 82, 172,
-    104, 160, 169, 114, 58, 57, 180, 188, 19, 84, 231, 215, 55, 56, 216, 2, 143, 89, 87, 18, 69, 67, 37, 35,
-    26, 62, 210, 164, 135, 208, 73, 209, 156, 153, 157, 122, 129, 60, 128, 98, 75, 61, 88, 59, 3, 66, 25, 5,
-    6, 90, 239, 68, 223, 40, 39, 161, 63, 38, 93, 101, 190, 121, 11, 159, 158, 192, 77, 118, 147, 165, 21, 4,
-    7, 8, 23, 28, 91, 30, 163, 142, 170, 117, 70, 139, 107, 137, 261, 22, 20, 126, 258, 263, 264, 42, 133, 15,
-    214, 12, 259, 27, 131, 124, 108, 213, 10, 243, 41, 262, 9, 260, 29, 162, 182, 96, 103, 24, 105, 44, 43,
-    132, 173, 244, 245, 16, 181, 116, 212, 97, 102, 14, 13, 95, 31, 45, 166, 246, 247, 221, 189, 222, 265,
-    270, 267, 268, 269, 272, 17, 271, 266, 138, 228, 219, 220, 130, 145, 109, 123, 226, 229, 146, 125, 248,
-    111, 249, 225, 120, 144, 218, 217, 230, 106, 99, 112, 110, 250, 224, 255, 184, 186, 251, 141, 256, 235,
-    236, 253, 252, 257, 254, 233, 234, 134, 276, 127, 277, 274, 275, 273, 183, 185, 191, 193, 148, 238, 237,
-    241, 113, 240, 278, 279, 242, 187, 194, 280, 283, 287, 285, 282, 284, 286, 281, 293, 288, 292, 324, 289,
-    325, 327, 329, 326, 290, 294, 306, 328, 308, 302, 295, 305, 309, 348, 333, 331, 338, 332, 342, 317, 330,
-    349, 353, 334, 350, 352, 335, 319, 316, 310, 351, 303, 313, 298, 323, 301, 320, 321, 318, 307, 304, 314,
-    296, 322, 355, 362, 354, 359, 358, 356, 366, 357, 337, 341, 336, 339, 311, 300, 360, 363, 361, 365, 343,
-    297, 315, 312, 340, 397, 400, 401, 399, 398, 347, 346, 345, 344, 299, 364, 367, 368, 372, 370, 369, 371,
-    373, 376, 377, 375, 374, 402, 407, 406, 404, 414, 403, 410, 405, 378, 383, 409, 413, 382, 380, 408, 411,
-    381, 379, 386, 390, 384, 387, 385, 389, 415, 412, 416, 418, 420, 417, 419, 388, 391, 392, 395, 396, 393,
-    394,
+    0, 32, 64, 93, 125, 157, 189, 218, 250, 266, 282, 2, 253, 1, 26, 268, 19, 94, 251, 34, 252, 112, 95, 118,
+    33, 244, 25, 50, 66, 119, 243, 111, 283, 254, 394, 267, 98, 99, 87, 3, 5, 6, 275, 7, 8, 101, 100, 36, 39,
+    40, 35, 38, 18, 37, 65, 104, 4, 42, 41, 116, 255, 57, 58, 261, 248, 70, 123, 68, 23, 21, 259, 51, 258, 28,
+    114, 286, 288, 271, 151, 12, 11, 27, 105, 52, 126, 272, 256, 262, 260, 44, 10, 144, 9, 257, 54, 30, 43,
+    91, 115, 122, 46, 108, 67, 72, 69, 29, 247, 45, 15, 13, 20, 158, 22, 47, 14, 49, 97, 109, 80, 48, 127, 17,
+    287, 16, 294, 143, 31, 274, 130, 128, 270, 131, 71, 205, 264, 265, 60, 62, 183, 73, 136, 96, 86, 263, 113,
+    79, 53, 55, 120, 74, 163, 160, 150, 153, 273, 155, 76, 162, 61, 59, 182, 24, 159, 146, 148, 129, 132, 133,
+    176, 140, 168, 103, 219, 102, 137, 82, 84, 246, 280, 278, 175, 172, 107, 106, 141, 117, 236, 134, 289,
+    135, 110, 207, 237, 209, 245, 63, 56, 197, 138, 139, 279, 220, 161, 165, 164, 145, 147, 75, 269, 77, 223,
+    224, 314, 316, 318, 313, 317, 315, 319, 301, 187, 295, 81, 298, 167, 229, 186, 152, 169, 185, 303, 249,
+    180, 178, 331, 343, 90, 89, 221, 121, 299, 226, 225, 149, 88, 284, 285, 328, 78, 179, 304, 83, 198, 302,
+    184, 222, 241, 204, 300, 276, 166, 171, 211, 191, 177, 277, 332, 212, 173, 230, 344, 320, 324, 322, 326,
+    321, 170, 327, 325, 323, 346, 85, 156, 190, 201, 345, 142, 238, 199, 347, 234, 233, 333, 124, 227, 228,
+    239, 334, 281, 174, 92, 240, 291, 290, 293, 292, 154, 305, 310, 307, 309, 311, 308, 312, 181, 188, 306,
+    329, 232, 330, 231, 361, 348, 358, 242, 206, 376, 297, 208, 200, 296, 363, 364, 195, 193, 216, 192, 194,
+    362, 349, 335, 340, 337, 341, 342, 336, 339, 338, 215, 359, 360, 214, 235, 213, 202, 377, 370, 368, 379,
+    367, 369, 372, 373, 378, 203, 388, 210, 371, 386, 387, 365, 350, 354, 196, 217, 380, 385, 355, 352, 351,
+    390, 391, 353, 356, 357, 389, 366, 374, 395, 381, 382, 392, 375, 397, 403, 402, 400, 383, 398, 401, 404,
+    409, 393, 399, 407, 411, 406, 405, 410, 408, 384, 396, 412, 422, 424, 425, 427, 420, 451, 413, 421, 415,
+    426, 428, 429, 423, 431, 418, 476, 480, 481, 478, 479, 505, 510, 509, 507, 508, 452, 455, 453, 454, 456,
+    417, 414, 430, 416, 419, 432, 506, 511, 513, 514, 512, 435, 460, 477, 484, 482, 485, 434, 483, 457, 462,
+    436, 433, 437, 438, 458, 465, 445, 459, 515, 520, 519, 518, 517, 527, 516, 523, 441, 469, 461, 486, 522,
+    491, 490, 526, 488, 498, 521, 524, 489, 487, 494, 439, 442, 464, 468, 440, 444, 463, 466, 493, 497, 492,
+    495, 528, 443, 525, 529, 532, 531, 533, 530, 470, 446, 448, 447, 467, 471, 474, 472, 475, 499, 496, 500,
+    502, 503, 504, 501, 473, 450, 449,
 )
-MESSAGES = 342
+MESSAGES = 427
 
 
 def wrap(value, count):
@@ -198,15 +203,17 @@
     return names + [(n, "s", d, sign) for d in OFFSETS for sign in "+-"]
 
 
-def add_weight(plan, g, n, cut, own, full, wide):
+def add_weight(plan, g, n, h, cut, own, full, wide):
     i = g.at(cut)
     needs = {e: [] for e in OFFSETS}
-    plan.load((n, "l"), own, full.at[i])
-    needs[0].append((n, "l"))
+    mine = pl.ds(h * HEAD_DIM, HEAD_DIM)
 
     def cutout(ref, start, size):
         rows = pl.ds(pl.multiple_of(start, 128), size)
-        return ref.at[:, rows] if wide else ref.at[rows]
+        return ref.at[mine, rows] if wide else ref.at[rows, mine]
+
+    plan.load((n, h, "l"), cutout(own, 0, NT * W), cutout(full.at[i], 0, NT * W))
+    needs[0].append((n, h, "l"))
 
     def add_piece(p, begin, size, shared):
         half = SIDE * size if shared else size
@@ -260,10 +267,10 @@
 
     begin = 0
     for count, size in enumerate(SHARES[n]):
-        add_piece((n, count), begin, size, True)
+        add_piece((n, h, count), begin, size, True)
         begin += 2 * SIDE * size
     while begin < NT * W:
-        add_piece((n, begin // (2 * ALONE) + 8), begin, ALONE, False)
+        add_piece((n, h, begin // (2 * ALONE) + 8), begin, ALONE, False)
         begin += 2 * ALONE
     return needs
 
@@ -272,8 +279,9 @@
     return jnp.concatenate(blocks, 1)
 
 
-def add_project(plan, g, n, cut, ring, buf, have, full, needs, wide, dst, sender):
+def add_project(plan, g, n, h, cut, ring, buf, have, full, needs, wide, dst, sender):
     i = g.at(cut)
+    mine = slice(h * HEAD_DIM, (h + 1) * HEAD_DIM)
 
     def columns(e):
         at = wrap(i + e, SIDE)
@@ -285,9 +293,9 @@
                 left = lanes([buf[k, m] for k in range(SIDE)])
             depth = pl.ds(m * SIDE * W, SIDE * W)
             if wide:
-                term = lax.dot_general(left, full[at, :, depth], NT_DIMS, preferred_element_type=F32)
+                term = lax.dot_general(left, full[at, mine, depth], NT_DIMS, preferred_element_type=F32)
             else:
-                term = jnp.dot(left, full[at, depth, :], preferred_element_type=F32)
+                term = jnp.dot(left, full[at, depth, mine], preferred_element_type=F32)
             total = term if total is None else total + term
         return total.astype(BF16)
 
@@ -301,29 +309,30 @@
         return work
 
     for e in OFFSETS:
-        plan.step((n, "p", e), make(e), tuple(have + needs[e]))
+        plan.step((n, h, "p", e), make(e), tuple(have + needs[e]))
         if e:
             plan.message(
-                (n, "o", e), sender.at[e], dst(i), g.along(cut, e), dst(wrap(i - e, SIDE)),
-                ((n, "p", e),),
-            )
-    return [(n, "p", 0)] + [(n, "o", e) for e in (1, 2, 3)]
-
-
-def add_scatter(plan, g, n, cut, ring, own, own_step, got, parts, one, two, make, out, old=(), final=None):
+                (n, h, "o", e), sender.at[e], dst(i), g.along(cut, e), dst(wrap(i - e, SIDE)),
+                ((n, h, "p", e),),
+            )
+    return [(n, h, "p", 0)] + [(n, h, "o", e) for e in (1, 2, 3)]
+
+
+def add_scatter(plan, g, n, cut, ring, swaps, parts, one, two, make, out, old=(), final=None):
     i, j = g.at(cut), g.at(ring)
-
-    def keep():
-        got[i] = own[i]
-
-    plan.step((n, "k"), keep, (own_step,))
-    for k in (1, 3, 2):
-        peer = wrap(i + k, SIDE)
-        plan.message(
-            (n, "x", k), own.at[peer], got.at[i], g.along(cut, k), got.at[wrap(i - k, SIDE)],
-            (own_step,),
-        )
-    swapped = ((n, "k"), (n, "x", 1), (n, "x", 2), (n, "x", 3))
+    swapped = ()
+    for count, (own, own_step, got) in enumerate(swaps):
+        def keep(own=own, got=got):
+            got[i] = own[i]
+
+        plan.step((n, "k", count), keep, (own_step,))
+        for k in (1, 3, 2):
+            peer = wrap(i + k, SIDE)
+            plan.message(
+                (n, "x", count, k), own.at[peer], got.at[i], g.along(cut, k), got.at[wrap(i - k, SIDE)],
+                (own_step,),
+            )
+        swapped += ((n, "k", count),) + tuple((n, "x", count, k) for k in (1, 2, 3))
 
     def part(dj, where=None):
         block = parts.at[wrap(j + dj, SIDE)]
@@ -393,48 +402,52 @@
     plan, g,
     enc_ref, hid_ref, gout_ref, wq_ref, wk_ref, wv_ref, wo_ref, rows_ref, slot_ref,
     out_ref, gh_ref, ge_ref,
-    enc_all, hid_all, gout_all, wq, wk, wv, wo, kv_send, q_send, ga_send, own_k, own_v, stage_k, stage_v,
-    k_in, v_in, q_ext, ga_ext, q_span, ga_span, probs, att, gq, tok_a, tok_c, got_a, got_c, reads,
-    slot_out, slot_in, gkv, gkv_t, gkv_got, parts_c, parts_enc, one_a, two_a, one_c, two_c, one_enc, two_enc,
+    enc_all, hid_all, gout_all, wq, wk, wv, wo, kv_send, q_send, ga_send, own_k0, own_k1, own_v0, own_v1,
+    stage_k, stage_v, k_in0, k_in1, v_in0, v_in1, q_ext, ga_ext, q_span, ga_span, probs, att, gq, tok_a, tok_c, got_a, got_c, reads,
+    slot_out, slot_in, gkv_t, gkv_got, parts_c, parts_enc, one_a, two_a, one_c, two_c, one_enc, two_enc,
     final_c, final_enc, chain,
 ):
     scale = HEAD_DIM ** (-0.5)
+    k_in, v_in = (k_in0, k_in1), (v_in0, v_in1)
     all_weights = {}
-    for n, cut, own, full in (("K", "x", wk_ref, wk), ("V", "x", wv_ref, wv), ("Q", "z", wq_ref, wq), ("O", "z", wo_ref, wo)):
-        all_weights[n] = add_weight(plan, g, n, cut, own, full, n == "O")
+    for h in range(HEADS):
+        for n, cut, own, full in (
+            ("K", "x", wk_ref, wk), ("V", "x", wv_ref, wv), ("Q", "z", wq_ref, wq), ("O", "z", wo_ref, wo)
+        ):
+            all_weights[n, h] = add_weight(plan, g, n, h, cut, own, full, n == "O")
     enc = add_gather(plan, g, "E", "x", "z", enc_ref, enc_all)
     hid = add_gather(plan, g, "H", "z", "x", hid_ref, hid_all)
     gout = add_gather(plan, g, "G", "z", "x", gout_ref, gout_all)
 
     per = EQ // RLEN
-    for n, full, own, stage, sender, land in (
-        ("K", wk, own_k, stage_k, kv_send.at[0], k_in), ("V", wv, own_v, stage_v, kv_send.at[1], v_in)
-    ):
-        def rows(i, own=own):
-            return own.at[pl.ds(i * per, per)]
-
-        made = add_project(
-            plan, g, n, "x", "z", enc_all, enc, full, all_weights[n], False, rows, sender
-        )
-
-        def pick(own=own, stage=stage, land=land):
-            @pl.loop(0, NSEQ)
-            def _(r):
-                for s in range(2):
-                    stage[r, s] = own[jnp.maximum(rows_ref[0, 2 * r + s], 0)]
-
-            land[g.seq] = stage[g.seq]
-
-        plan.step((n, "x"), pick, tuple(made))
-        for k in range(1, NSEQ):
-            plan.message(
-                (n, "a", k), stage.at[wrap(g.seq + k, NSEQ)], land.at[g.seq], g.along("seq", k),
-                land.at[wrap(g.seq - k, NSEQ)], ((n, "x"),),
-            )
+    for h in range(HEADS):
+        for n, full, own, stage, sender, land in (
+            ("K", wk, (own_k0, own_k1)[h], stage_k.at[h], kv_send.at[0, h], k_in[h]),
+            ("V", wv, (own_v0, own_v1)[h], stage_v.at[h], kv_send.at[1, h], v_in[h]),
+        ):
+            def rows(i, own=own):
+                return own.at[pl.ds(i * per, per)]
+
+            made = add_project(
+                plan, g, n, h, "x", "z", enc_all, enc, full, all_weights[n, h], False, rows, sender
+            )
+
+            def pick(own=own, stage=stage, land=land):
+                @pl.loop(0, NSEQ)
+                def _(r):
+                    for s in range(2):
+                        stage[r, s] = own[jnp.maximum(rows_ref[0, 2 * r + s], 0)]
+
+                land[g.seq] = stage[g.seq]
+
+            plan.step((n, h, "x"), pick, tuple(made))
+            for k in range(1, NSEQ):
+                plan.message(
+                    (n, h, "a", k), stage.at[wrap(g.seq + k, NSEQ)], land.at[g.seq], g.along("seq", k),
+                    land.at[wrap(g.seq - k, NSEQ)], ((n, h, "x"),),
+                )
 
     head, tail = pl.ds(0, SPAN), pl.ds(ROWS, SPAN)
-    row = col = None
-
     def shift_rows(by, limit=None):
         row = lax.broadcasted_iota(jnp.int32, (Q, Q + SPAN), 0)
         col = lax.broadcasted_iota(jnp.int32, (Q, Q + SPAN), 1)
@@ -443,36 +456,38 @@
             picked = jnp.logical_and(picked, col < limit)
         return picked.astype(BF16)
 
-    for n, buf, have, full, ext, span, sender in (
-        ("Q", hid_all, hid, wq, q_ext, q_span, q_send), ("O", gout_all, gout, wo, ga_ext, ga_span, ga_send)
-    ):
-        def rows(i, ext=ext):
-            return ext.at[pl.ds(pl.multiple_of(i * Q, Q), Q)]
-
-        made = add_project(
-            plan, g, n, "z", "x", buf, have, full, all_weights[n], n == "O", rows, sender
-        )
-        plan.message(
-            (n, "e"), ext.at[head], ext.at[tail], g.along("seq", NSEQ - 1), ext.at[tail], tuple(made)
-        )
-
-        def align(ext=ext, span=span):
-            for m in range(SIDE):
-                limit = None
-                if m == SIDE - 1:
-                    limit = jnp.where(g.seq == NSEQ - 1, Q, Q + SPAN)
-                moved = jnp.dot(
-                    shift_rows(SPAN - 1, limit), ext[m * Q : (m + 1) * Q + SPAN, :],
-                    preferred_element_type=F32,
-                )
-                span[m * Q : (m + 1) * Q, :] = moved.astype(BF16)
-
-        plan.step((n, "t"), align, tuple(made) + ((n, "e"),))
+    for h in range(HEADS):
+        for n, buf, have, full, ext, span, sender in (
+            ("Q", hid_all, hid, wq, q_ext.at[h], q_span.at[h], q_send.at[h]),
+            ("O", gout_all, gout, wo, ga_ext.at[h], ga_span.at[h], ga_send.at[h]),
+        ):
+            def rows(i, ext=ext):
+                return ext.at[pl.ds(pl.multiple_of(i * Q, Q), Q)]
+
+            made = add_project(
+                plan, g, n, h, "z", "x", buf, have, full, all_weights[n, h], n == "O", rows, sender
+            )
+            plan.message(
+                (n, h, "e"), ext.at[head], ext.at[tail], g.along("seq", NSEQ - 1), ext.at[tail], tuple(made)
+            )
+
+            def align(ext=ext, span=span):
+                for m in range(SIDE):
+                    limit = None
+                    if m == SIDE - 1:
+                        limit = jnp.where(g.seq == NSEQ - 1, Q, Q + SPAN)
+                    moved = jnp.dot(
+                        shift_rows(SPAN - 1, limit), ext[m * Q : (m + 1) * Q + SPAN, :],
+                        preferred_element_type=F32,
+                    )
+                    span[m * Q : (m + 1) * Q, :] = moved.astype(BF16)
+
+            plan.step((n, h, "t"), align, tuple(made) + ((n, h, "e"),))
 
     def tables():
         for kind in range(2):
             reads[kind, NONE] = jnp.zeros((RLEN, HEAD_DIM), F32)
-        ids = [slot_ref[p // NEIGH, p % NEIGH] for p in range(NONE)]
+        ids = [slot_ref[p % NEIGH, p // NEIGH] for p in range(NONE)]
         targets = [rows_ref[0, j] for j in range(NONE)]
         for line, values in ((0, ids), (2, targets)):
             for p in range(NONE):
@@ -486,11 +501,11 @@
 
     plan.step(("T", "t"), tables)
 
-    def read(ref, u, cols):
+    def read(ref, u):
         picked = []
         for j in range(NEIGH):
-            s = slot_ref[u, j]
-            picked.append(ref[lax.div(s, 2), lax.rem(s, 2), :, cols])
+            s = slot_ref[j, u]
+            picked.append(ref[lax.div(s, 2), lax.rem(s, 2)])
         return jnp.concatenate(picked, 0)
 
     def forward(h):
@@ -500,9 +515,9 @@
             @pl.loop(0, SPANS, unroll=UNROLL)
             def _(u):
                 here = pl.ds(pl.multiple_of(u * SPAN, SPAN), SPAN)
-                k, v = read(k_in, u, cols), read(v_in, u, cols)
+                k, v = read(k_in[h], u), read(v_in[h], u)
                 scores = lax.dot_general(
-                    q_span[here, cols], k, NT_DIMS, preferred_element_type=F32
+                    q_span[h, here, :], k, NT_DIMS, preferred_element_type=F32
                 ) * scale
                 peak = jnp.max(scores, axis=-1, keepdims=True)
                 weights = jnp.exp(scores - peak)
@@ -520,9 +535,9 @@
             @pl.loop(0, SPANS, unroll=UNROLL)
             def _(u):
                 here = pl.ds(pl.multiple_of(u * SPAN, SPAN), SPAN)
-                k, v = read(k_in, u, cols), read(v_in, u, cols)
+                k, v = read(k_in[h], u), read(v_in[h], u)
                 prob = probs[h, u]
-                q, gr = q_span[here, cols], ga_span[here, cols]
+                q, gr = q_span[h, here, :], ga_span[h, here, :]
                 grad_probs = lax.dot_general(gr, v, NT_DIMS, preferred_element_type=F32)
                 dot_sum = jnp.sum(grad_probs * prob, axis=-1, keepdims=True)
                 grad_scores = (prob * (grad_probs - dot_sum) * scale).astype(BF16)
@@ -553,11 +568,12 @@
 
         return work
 
-    landed = tuple((n, "a", k) for n in "KV" for k in range(1, NSEQ)) + (("K", "x"), ("V", "x"))
     for h in range(HEADS):
-        plan.step(("F", h), forward(h), landed + (("Q", "t"),))
+        landed = tuple((n, h, "a", k) for n in "KV" for k in range(1, NSEQ))
+        landed += tuple((n, h, "x") for n in "KV")
+        plan.step(("F", h), forward(h), landed + (("Q", h, "t"),))
     for h in range(HEADS):
-        plan.step(("B", h), backward(h), (("F", h), ("O", "t"), ("T", "t")))
+        plan.step(("B", h), backward(h), (("F", h), ("O", h, "t"), ("T", "t")))
         for r in range(2):
             for k in range(1, NSEQ):
                 plan.message(
@@ -605,33 +621,27 @@
             return result.at[pl.ds(pl.multiple_of(i * Q, Q), Q)]
 
         add_scatter(
-            plan, g, n, "z", "x", tok, (n, "t"), got, parts, one, two, make, rows, old, final
+            plan, g, n, "z", "x", ((tok, (n, "t"), got),), parts, one, two, make, rows, old, final
         )
 
-    def owner_sums(r):
+    def owner_sums(r, h):
         def work():
+            rows = slice(h * HALF, (h + 1) * HALF)
+
             @pl.loop(0, NSEQ)
             def _(o):
                 for slot in range(2):
                     p = 2 * o + slot
                     before = chain[2, p]
                     for kind in range(2):
-                        for h in range(HEADS):
-                            rows = slice(h * HALF, (h + 1) * HALF)
-                            value = slot_in[h, r, o, slot, kind].astype(F32)
-                            reads[kind, p, rows, :] = value + reads[kind, before, rows, :]
-
-            for n in range(NSEQ):
-                latest = chain[3, n]
-                for kind in range(2):
-                    for h in range(HEADS):
-                        rows = slice(h * HALF, (h + 1) * HALF)
-                        cols = slice(h * HEAD_DIM, (h + 1) * HEAD_DIM)
-                        place = slice((n % per) * HALF, (n % per + 1) * HALF)
-                        gkv[n // per, kind, place, cols] = reads[kind, latest, rows, :].astype(BF16)
+                        value = slot_in[h, r, o, slot, kind].astype(F32)
+                        reads[kind, p, rows, :] = value + reads[kind, before, rows, :]
+
             for k in range(SIDE):
                 for kind in range(2):
-                    gkv_t[r, k, kind] = gkv[k, kind].astype(F32).T.astype(BF16)
+                    owned = [reads[kind, chain[3, k * per + m], rows, :] for m in range(per)]
+                    total = jnp.concatenate(owned, 0).astype(BF16).astype(F32)
+                    gkv_t[r, h, k, kind] = total.T.astype(BF16)
 
         return work
 
@@ -641,23 +651,24 @@
             total = None
             for kind, w in ((0, wk), (1, wv)):
                 for k in range(SIDE):
-                    term = jnp.dot(
-                        w[k, depth, :], gkv_got[r, k, kind], preferred_element_type=F32
-                    )
+                    right = jnp.concatenate([gkv_got[r, h, k, kind] for h in range(HEADS)], 0)
+                    term = jnp.dot(w[k, depth, :], right, preferred_element_type=F32)
                     total = term if total is None else total + term
             return total
 
         return make
 
     for r in range(2):
-        came = tuple(("S", h, r, "a", k) for h in range(HEADS) for k in range(1, NSEQ))
-        plan.step(("W", r), owner_sums(r), came + (("B", 0), ("B", 1)))
+        for h in range(HEADS):
+            came = tuple(("S", h, r, "a", k) for k in range(1, NSEQ))
+            plan.step(("W", h, r), owner_sums(r, h), came + (("B", h),))
 
         def rows(i, r=r):
             return ge_ref.at[pl.ds(i * per, per), pl.ds(r * HALF, HALF)]
 
         add_scatter(
-            plan, g, ("Y", r), "x", "z", gkv_t.at[r], ("W", r), gkv_got.at[r], parts_enc.at[r],
+            plan, g, ("Y", r), "x", "z",
+            [(gkv_t.at[r, h], ("W", h, r), gkv_got.at[r, h]) for h in range(HEADS)], parts_enc.at[r],
             one_enc.at[r], two_enc.at[r], enc_part(r), rows, (), final_enc.at[r],
         )
 
@@ -681,19 +692,22 @@
 
     weight = vmem(SIDE, NT * W, W)
     quarters = vmem(SIDE, Q, W)
+    by_head = vmem(HEADS, SIDE, Q, HEAD_DIM)
+    owned, came = vmem(NSEQ, RLEN, HEAD_DIM), vmem(NSEQ, 2, RLEN, HEAD_DIM)
+    tokens = vmem(HEADS, ROWS + SPAN, HEAD_DIM)
     return [
         vmem(SIDE, SIDE, EQ, W), vmem(SIDE, SIDE, Q, W), vmem(SIDE, SIDE, Q, W),
         weight, weight, weight, vmem(SIDE, W, NT * W),
-        vmem(2, SIDE, EQ // RLEN, RLEN, W), quarters, quarters,
-        vmem(NSEQ, RLEN, W), vmem(NSEQ, RLEN, W),
-        vmem(NSEQ, 2, RLEN, W), vmem(NSEQ, 2, RLEN, W), vmem(NSEQ, 2, RLEN, W), vmem(NSEQ, 2, RLEN, W),
-        vmem(ROWS + SPAN, W), vmem(ROWS + SPAN, W), vmem(ROWS, W), vmem(ROWS, W),
+        vmem(2, HEADS, SIDE, EQ // RLEN, RLEN, HEAD_DIM), by_head, by_head,
+        owned, owned, owned, owned,
+        vmem(HEADS, NSEQ, 2, RLEN, HEAD_DIM), vmem(HEADS, NSEQ, 2, RLEN, HEAD_DIM), came, came, came, came,
+        tokens, tokens, vmem(HEADS, ROWS, HEAD_DIM), vmem(HEADS, ROWS, HEAD_DIM),
         vmem(HEADS, SPANS, SPAN, NEIGH * RLEN, dtype=F32),
         vmem(ROWS + SPAN, W), vmem(ROWS + SPAN, W),
         quarters, vmem(SIDE, W, Q), quarters, vmem(SIDE, W, Q),
         vmem(2, NONE + 1, RLEN, HEAD_DIM, dtype=F32),
         vmem(HEADS, 2, NSEQ, 2, 2, HALF, HEAD_DIM), vmem(HEADS, 2, NSEQ, 2, 2, HALF, HEAD_DIM),
-        vmem(SIDE, 2, Q, W), vmem(2, SIDE, 2, W, Q), vmem(2, SIDE, 2, W, Q),
+        vmem(2, HEADS, SIDE, 2, HEAD_DIM, Q), vmem(2, HEADS, SIDE, 2, HEAD_DIM, Q),
         vmem(SIDE, SIDE, W, Q), vmem(2, SIDE, SIDE, W, Q),
         vmem(2, 2, Q, W), vmem(2, SIDE, Q, W), vmem(2, 2, W, Q), vmem(2, SIDE, W, Q),
         vmem(2, 2, 2, W, Q), vmem(2, 2, SIDE, W, Q),
@@ -705,22 +719,41 @@
     return jax.ShapeDtypeStruct(dims, dtype)
 
 
+def hand_over(*refs):
+    *pairs, sem = refs
+    copies = [
+        pltpu.make_async_copy(src, dst, sem.at[k]) for k, (src, dst) in enumerate(zip(pairs[:3], pairs[3:]))
+    ]
+    for copy in copies:
+        copy.start()
+    for copy in copies:
+        copy.wait()
+
+
 def per_device(hidden, encoded, w_query, w_key, w_value, w_out, send_rows, read_slot, grad_out):
     dma = pltpu.SemaphoreType.DMA
-    out, gh, ge = pl.pallas_call(
+    shapes = (shape(ROWS, W), shape(ROWS, W), shape(NSEQ, RLEN, W))
+    results = pl.pallas_call(
         kernel,
         name="cross_attention",
-        out_shape=(shape(ROWS, W), shape(ROWS, W), shape(NSEQ, RLEN, W)),
+        out_shape=shapes,
         in_specs=[ANY] * 7 + [SM, SM],
         out_specs=(VM, VM, VM),
-        scratch_shapes=scratch() + [dma((MESSAGES,)), dma((MESSAGES,)), dma((7,))],
+        scratch_shapes=scratch() + [dma((MESSAGES,)), dma((MESSAGES,)), dma((11,))],
         compiler_params=pltpu.CompilerParams(
             collective_id=0, has_side_effects=True, vmem_limit_bytes=63 * 1024 * 1024
         ),
     )(
-        encoded.reshape(2 * ROWS, W), hidden, grad_out, w_query, w_key, w_value, w_out, send_rows, read_slot,
+        encoded.reshape(2 * ROWS, W), hidden, grad_out, w_query, w_key, w_value, w_out, send_rows, read_slot.T,
     )
-    return out, gh, ge
+    return pl.pallas_call(
+        hand_over,
+        name="hand_over",
+        out_shape=shapes,
+        in_specs=[ANY] * 3,
+        out_specs=(ANY,) * 3,
+        scratch_shapes=[dma((3,))],
+    )(*results)
 
 
 def solution(mesh):

time: 187 us -> 215 us (1.15)
  Pallas kernels: 179 us -> 213 us
  local copies, waits for them, and re-layouts: 6.55 us -> 0 us
    pallas_call x1 -> x2, Pallas kernels: 179 us -> 213 us  [the longest x1 180 us: per_device(): pl.pallas_call(kernel, name='cross_attention', out_shape=shapes, in_specs...]
    unnamed x4 -> x0, local copies, waits for them, and re-layouts: 6.55 us -> none
where the time goes in v4:
time: 215 us; the launch traced here: 214 us
  Pallas kernels  213 us (99%)
    pallas_call x1, Pallas kernels, per_device(): pl.pallas_call(kernel, name='cross_attention', out_shape=shapes, in_specs...  180 us
    pallas_call x1, Pallas kernels, per_device(): pl.pallas_call(hand_over, name='hand_over', out_shape=shapes, in_specs=[A...  32.9 us

profile of v4, /device:TPU:0, one launch (start us, length us, event | category | flops | bytes accessed | tf_op | source)
XLA Modules:
  0.0 213.7 jit_solution(12361751777612934814)
XLA Ops:
  0.6 180.0 %cross_attention.1 = (bf16[512,256]{1,0:T(8,128)(2,1)}, bf16[512,256]{1,0:T(8,128)(2,1)}, bf16[8,128,256]{2,1,0:T(8,128)(2,1)}) custom-call(bf16[1024,256]{1,0:T(8,128)(2,1)} %bitcast.2, bf16[512,256]{1,0:T(8,128)(2,1)} %refs_1_.1, bf16[512,256]{1,0:T(8,128)(2,1)} %refs_2_.1, bf16[4096,256]{1,0:T(8,128)(2,1)} %refs_3_.1, bf16[4096,256]{1,0:T(8,128)(2,1)} %refs_4_.1, ...), custom_call_target="tpu_custom_call" | custom-call | tf_op jit(solution)/shard_map/cross_attention/pallas_call | solution.py:736
  180.6 32.9 %hand_over.1 = (bf16[512,256]{1,0:T(8,128)(2,1)}, bf16[512,256]{1,0:T(8,128)(2,1)}, bf16[8,128,256]{2,1,0:T(8,128)(2,1)}) custom-call(bf16[512,256]{1,0:T(8,128)(2,1)} %get-tuple-element.6.refs_0_, bf16[512,256]{1,0:T(8,128)(2,1)} %get-tuple-element.7.refs_1_, bf16[8,128,256]{2,1,0:T(8,128)(2,1)} %get-tuple-element.8.refs_2_), custom_call_target="tpu_custom_call" | custom-call | tf_op jit(solution)/shard_map/hand_over/pallas_call | solution.py:749

commit v5 on v3

--- a/solution.py
+++ b/solution.py
@@ -32,34 +32,33 @@
 HALF = RLEN // 2
 NONE = SPANS * NEIGH
 OFFSETS = (0, 3, 1, 2)
-SHARES = {"K": (256,), "V": (256,), "Q": (), "O": (256,)}
+SHARES = {"K": (256, 256), "V": (256,), "Q": (256,), "O": ()}
 ALONE = 256
 UNROLL = 2
 
 
 ORDER = (
-    0, 46, 92, 149, 195, 211, 227, 199, 200, 197, 198, 175, 115, 196, 167, 174, 136, 168, 100, 150, 32, 78,
-    48, 47, 79, 72, 291, 207, 65, 85, 33, 204, 71, 205, 206, 119, 203, 155, 177, 36, 34, 202, 154, 76, 83,
-    140, 176, 201, 74, 81, 80, 152, 49, 151, 94, 50, 51, 54, 53, 1, 64, 86, 232, 52, 178, 171, 179, 82, 172,
-    104, 160, 169, 114, 58, 57, 180, 188, 19, 84, 231, 215, 55, 56, 216, 2, 143, 89, 87, 18, 69, 67, 37, 35,
-    26, 62, 210, 164, 135, 208, 73, 209, 156, 153, 157, 122, 129, 60, 128, 98, 75, 61, 88, 59, 3, 66, 25, 5,
-    6, 90, 239, 68, 223, 40, 39, 161, 63, 38, 93, 101, 190, 121, 11, 159, 158, 192, 77, 118, 147, 165, 21, 4,
-    7, 8, 23, 28, 91, 30, 163, 142, 170, 117, 70, 139, 107, 137, 261, 22, 20, 126, 258, 263, 264, 42, 133, 15,
-    214, 12, 259, 27, 131, 124, 108, 213, 10, 243, 41, 262, 9, 260, 29, 162, 182, 96, 103, 24, 105, 44, 43,
-    132, 173, 244, 245, 16, 181, 116, 212, 97, 102, 14, 13, 95, 31, 45, 166, 246, 247, 221, 189, 222, 265,
-    270, 267, 268, 269, 272, 17, 271, 266, 138, 228, 219, 220, 130, 145, 109, 123, 226, 229, 146, 125, 248,
-    111, 249, 225, 120, 144, 218, 217, 230, 106, 99, 112, 110, 250, 224, 255, 184, 186, 251, 141, 256, 235,
-    236, 253, 252, 257, 254, 233, 234, 134, 276, 127, 277, 274, 275, 273, 183, 185, 191, 193, 148, 238, 237,
-    241, 113, 240, 278, 279, 242, 187, 194, 280, 283, 287, 285, 282, 284, 286, 281, 293, 288, 292, 324, 289,
-    325, 327, 329, 326, 290, 294, 306, 328, 308, 302, 295, 305, 309, 348, 333, 331, 338, 332, 342, 317, 330,
-    349, 353, 334, 350, 352, 335, 319, 316, 310, 351, 303, 313, 298, 323, 301, 320, 321, 318, 307, 304, 314,
-    296, 322, 355, 362, 354, 359, 358, 356, 366, 357, 337, 341, 336, 339, 311, 300, 360, 363, 361, 365, 343,
-    297, 315, 312, 340, 397, 400, 401, 399, 398, 347, 346, 345, 344, 299, 364, 367, 368, 372, 370, 369, 371,
-    373, 376, 377, 375, 374, 402, 407, 406, 404, 414, 403, 410, 405, 378, 383, 409, 413, 382, 380, 408, 411,
-    381, 379, 386, 390, 384, 387, 385, 389, 415, 412, 416, 418, 420, 417, 419, 388, 391, 392, 395, 396, 393,
-    394,
+    0, 35, 81, 127, 184, 200, 216, 2, 185, 1, 19, 113, 18, 114, 188, 136, 280, 129, 106, 186, 4, 7, 8, 25,
+    117, 115, 205, 21, 24, 116, 196, 53, 5, 191, 3, 187, 192, 110, 133, 131, 193, 6, 140, 75, 118, 190, 119,
+    22, 54, 12, 60, 29, 164, 57, 55, 9, 82, 11, 23, 74, 198, 197, 221, 195, 194, 79, 77, 37, 28, 64, 58, 62,
+    204, 20, 56, 16, 166, 10, 68, 67, 163, 78, 33, 86, 87, 13, 120, 189, 108, 199, 138, 14, 15, 36, 61, 26,
+    212, 27, 39, 42, 70, 72, 168, 32, 69, 43, 76, 92, 177, 201, 100, 217, 17, 165, 218, 220, 235, 233, 232,
+    124, 47, 71, 167, 107, 63, 236, 38, 40, 234, 31, 41, 224, 228, 65, 83, 202, 59, 207, 80, 84, 30, 225, 247,
+    169, 156, 96, 142, 223, 128, 46, 66, 181, 34, 102, 44, 206, 45, 109, 150, 230, 208, 209, 88, 85, 89, 213,
+    222, 111, 237, 238, 51, 229, 121, 99, 49, 144, 146, 50, 250, 135, 93, 251, 90, 91, 48, 143, 214, 132, 160,
+    73, 248, 249, 152, 154, 130, 104, 112, 239, 245, 241, 242, 101, 219, 103, 123, 240, 125, 94, 246, 52, 137,
+    95, 203, 122, 145, 178, 139, 134, 147, 252, 253, 157, 149, 226, 227, 105, 97, 244, 243, 170, 211, 210, 98,
+    158, 171, 231, 254, 256, 260, 255, 126, 180, 215, 259, 141, 151, 179, 271, 257, 153, 182, 159, 261, 161,
+    267, 268, 262, 263, 264, 265, 266, 173, 174, 175, 155, 172, 258, 183, 272, 273, 274, 275, 162, 148, 269,
+    176, 276, 277, 270, 281, 278, 282, 313, 279, 298, 303, 302, 299, 301, 304, 314, 317, 309, 318, 300, 283,
+    337, 289, 306, 284, 291, 315, 316, 311, 338, 340, 342, 288, 341, 287, 290, 339, 285, 308, 286, 319, 323,
+    322, 324, 305, 320, 327, 321, 331, 343, 346, 345, 294, 355, 344, 310, 325, 328, 307, 296, 362, 326, 366,
+    330, 293, 295, 363, 292, 312, 364, 297, 365, 329, 386, 387, 347, 389, 388, 332, 334, 333, 336, 367, 371,
+    372, 335, 390, 368, 369, 379, 370, 348, 375, 351, 374, 373, 391, 395, 396, 378, 376, 393, 403, 392, 399,
+    394, 350, 354, 349, 352, 397, 400, 398, 402, 380, 377, 381, 384, 385, 383, 382, 356, 353, 357, 361, 358,
+    360, 359, 401, 404, 405, 408, 407, 409, 406,
 )
-MESSAGES = 342
+MESSAGES = 331
 
 
 def wrap(value, count):
@@ -472,7 +471,7 @@
     def tables():
         for kind in range(2):
             reads[kind, NONE] = jnp.zeros((RLEN, HEAD_DIM), F32)
-        ids = [slot_ref[p // NEIGH, p % NEIGH] for p in range(NONE)]
+        ids = [slot_ref[p % NEIGH, p // NEIGH] for p in range(NONE)]
         targets = [rows_ref[0, j] for j in range(NONE)]
         for line, values in ((0, ids), (2, targets)):
             for p in range(NONE):
@@ -489,7 +488,7 @@
     def read(ref, u, cols):
         picked = []
         for j in range(NEIGH):
-            s = slot_ref[u, j]
+            s = slot_ref[j, u]
             picked.append(ref[lax.div(s, 2), lax.rem(s, 2), :, cols])
         return jnp.concatenate(picked, 0)
 
@@ -705,12 +704,18 @@
     return jax.ShapeDtypeStruct(dims, dtype)
 
 
+def hand_over(*refs):
+    for src, dst in zip(refs[:3], refs[3:]):
+        dst[...] = src[...]
+
+
 def per_device(hidden, encoded, w_query, w_key, w_value, w_out, send_rows, read_slot, grad_out):
     dma = pltpu.SemaphoreType.DMA
-    out, gh, ge = pl.pallas_call(
+    shapes = (shape(ROWS, W), shape(ROWS, W), shape(NSEQ, RLEN, W))
+    results = pl.pallas_call(
         kernel,
         name="cross_attention",
-        out_shape=(shape(ROWS, W), shape(ROWS, W), shape(NSEQ, RLEN, W)),
+        out_shape=shapes,
         in_specs=[ANY] * 7 + [SM, SM],
         out_specs=(VM, VM, VM),
         scratch_shapes=scratch() + [dma((MESSAGES,)), dma((MESSAGES,)), dma((7,))],
@@ -718,9 +723,15 @@
             collective_id=0, has_side_effects=True, vmem_limit_bytes=63 * 1024 * 1024
         ),
     )(
-        encoded.reshape(2 * ROWS, W), hidden, grad_out, w_query, w_key, w_value, w_out, send_rows, read_slot,
+        encoded.reshape(2 * ROWS, W), hidden, grad_out, w_query, w_key, w_value, w_out, send_rows, read_slot.T,
     )
-    return out, gh, ge
+    return pl.pallas_call(
+        hand_over,
+        name="hand_over",
+        out_shape=shapes,
+        in_specs=[VM] * 3,
+        out_specs=(VM,) * 3,
+    )(*results)
 
 
 def solution(mesh):

time: 187 us -> 174 us (0.930)
  local copies, waits for them, and re-layouts: 6.55 us -> 0 us
  Pallas kernels: 179 us -> 173 us
    unnamed x4 -> x0, local copies, waits for them, and re-layouts: 6.55 us -> none
    pallas_call x1 -> x2, Pallas kernels: 179 us -> 173 us  [the longest x1 171 us: per_device(): pl.pallas_call(kernel, name='cross_attention', out_shape=shapes, in_specs...]
where the time goes in v5:
time: 174 us
  Pallas kernels  173 us (99%)
    pallas_call x1, Pallas kernels, per_device(): pl.pallas_call(kernel, name='cross_attention', out_shape=shapes, in_specs...  171 us

profile of v5, /device:TPU:0, one launch (start us, length us, event | category | flops | bytes accessed | tf_op | source)
XLA Modules:
  0.0 173.5 jit_solution(17218842042552640998)
XLA Ops:
  0.6 170.7 %cross_attention.1 = (bf16[512,256]{1,0:T(8,128)(2,1)}, bf16[512,256]{1,0:T(8,128)(2,1)}, bf16[8,128,256]{2,1,0:T(8,128)(2,1)}) custom-call(bf16[1024,256]{1,0:T(8,128)(2,1)} %bitcast.2, bf16[512,256]{1,0:T(8,128)(2,1)} %refs_1_.1, bf16[512,256]{1,0:T(8,128)(2,1)} %refs_2_.1, bf16[4096,256]{1,0:T(8,128)(2,1)} %refs_3_.1, bf16[4096,256]{1,0:T(8,128)(2,1)} %refs_4_.1, ...), custom_call_target="tpu_custom_call" | custom-call | tf_op jit(solution)/shard_map/cross_attention/pallas_call | solution.py:715
  171.3 2.2 %hand_over.1 = (bf16[512,256]{1,0:T(8,128)(2,1)}, bf16[512,256]{1,0:T(8,128)(2,1)}, bf16[8,128,256]{2,1,0:T(8,128)(2,1)}) custom-call(bf16[512,256]{1,0:T(8,128)(2,1)} %get-tuple-element.6.refs_0_, bf16[512,256]{1,0:T(8,128)(2,1)} %get-tuple-element.7.refs_1_, bf16[8,128,256]{2,1,0:T(8,128)(2,1)} %get-tuple-element.8.refs_2_), custom_call_target="tpu_custom_call" | custom-call | tf_op jit(solution)/shard_map/hand_over/pallas_call | solution.py:728

commit v6 on v5

--- a/solution.py
+++ b/solution.py
@@ -38,25 +38,25 @@
 
 
 ORDER = (
-    0, 35, 81, 127, 184, 200, 216, 2, 185, 1, 19, 113, 18, 114, 188, 136, 280, 129, 106, 186, 4, 7, 8, 25,
-    117, 115, 205, 21, 24, 116, 196, 53, 5, 191, 3, 187, 192, 110, 133, 131, 193, 6, 140, 75, 118, 190, 119,
-    22, 54, 12, 60, 29, 164, 57, 55, 9, 82, 11, 23, 74, 198, 197, 221, 195, 194, 79, 77, 37, 28, 64, 58, 62,
-    204, 20, 56, 16, 166, 10, 68, 67, 163, 78, 33, 86, 87, 13, 120, 189, 108, 199, 138, 14, 15, 36, 61, 26,
-    212, 27, 39, 42, 70, 72, 168, 32, 69, 43, 76, 92, 177, 201, 100, 217, 17, 165, 218, 220, 235, 233, 232,
-    124, 47, 71, 167, 107, 63, 236, 38, 40, 234, 31, 41, 224, 228, 65, 83, 202, 59, 207, 80, 84, 30, 225, 247,
-    169, 156, 96, 142, 223, 128, 46, 66, 181, 34, 102, 44, 206, 45, 109, 150, 230, 208, 209, 88, 85, 89, 213,
-    222, 111, 237, 238, 51, 229, 121, 99, 49, 144, 146, 50, 250, 135, 93, 251, 90, 91, 48, 143, 214, 132, 160,
-    73, 248, 249, 152, 154, 130, 104, 112, 239, 245, 241, 242, 101, 219, 103, 123, 240, 125, 94, 246, 52, 137,
-    95, 203, 122, 145, 178, 139, 134, 147, 252, 253, 157, 149, 226, 227, 105, 97, 244, 243, 170, 211, 210, 98,
-    158, 171, 231, 254, 256, 260, 255, 126, 180, 215, 259, 141, 151, 179, 271, 257, 153, 182, 159, 261, 161,
-    267, 268, 262, 263, 264, 265, 266, 173, 174, 175, 155, 172, 258, 183, 272, 273, 274, 275, 162, 148, 269,
-    176, 276, 277, 270, 281, 278, 282, 313, 279, 298, 303, 302, 299, 301, 304, 314, 317, 309, 318, 300, 283,
-    337, 289, 306, 284, 291, 315, 316, 311, 338, 340, 342, 288, 341, 287, 290, 339, 285, 308, 286, 319, 323,
-    322, 324, 305, 320, 327, 321, 331, 343, 346, 345, 294, 355, 344, 310, 325, 328, 307, 296, 362, 326, 366,
-    330, 293, 295, 363, 292, 312, 364, 297, 365, 329, 386, 387, 347, 389, 388, 332, 334, 333, 336, 367, 371,
-    372, 335, 390, 368, 369, 379, 370, 348, 375, 351, 374, 373, 391, 395, 396, 378, 376, 393, 403, 392, 399,
-    394, 350, 354, 349, 352, 397, 400, 398, 402, 380, 377, 381, 384, 385, 383, 382, 356, 353, 357, 361, 358,
-    360, 359, 401, 404, 405, 408, 407, 409, 406,
+    0, 35, 81, 127, 184, 200, 216, 219, 99, 18, 106, 218, 1, 164, 107, 2, 280, 187, 19, 82, 171, 4, 7, 8, 20,
+    22, 23, 113, 3, 110, 108, 60, 103, 5, 6, 185, 168, 109, 166, 100, 111, 227, 21, 54, 120, 186, 195, 175,
+    188, 53, 86, 12, 112, 115, 28, 117, 87, 202, 11, 25, 37, 62, 64, 74, 190, 124, 102, 104, 191, 56, 199,
+    201, 55, 196, 67, 75, 57, 58, 16, 92, 27, 39, 114, 205, 9, 32, 10, 61, 24, 29, 192, 36, 101, 206, 59, 78,
+    15, 197, 69, 163, 76, 189, 31, 26, 96, 207, 77, 68, 194, 116, 226, 63, 79, 118, 13, 198, 65, 14, 43, 42,
+    220, 204, 33, 208, 38, 41, 224, 83, 165, 30, 40, 193, 213, 173, 209, 80, 167, 119, 225, 122, 142, 17, 70,
+    221, 228, 47, 84, 212, 170, 169, 34, 214, 157, 45, 44, 230, 231, 46, 89, 85, 88, 235, 236, 66, 237, 232,
+    73, 121, 72, 238, 51, 247, 144, 217, 91, 150, 159, 149, 233, 172, 234, 174, 161, 250, 251, 49, 146, 48,
+    93, 105, 71, 90, 50, 123, 129, 128, 222, 223, 239, 241, 95, 243, 176, 125, 52, 248, 249, 203, 143, 151,
+    229, 156, 94, 154, 97, 246, 252, 253, 245, 130, 131, 152, 133, 132, 153, 136, 271, 211, 210, 135, 244,
+    240, 126, 98, 242, 145, 177, 254, 215, 158, 256, 134, 147, 160, 260, 178, 261, 155, 255, 265, 263, 267,
+    264, 137, 268, 139, 259, 148, 138, 140, 262, 257, 266, 162, 179, 181, 180, 182, 272, 258, 274, 275, 273,
+    141, 269, 183, 276, 277, 270, 281, 278, 282, 313, 279, 298, 302, 305, 314, 316, 318, 317, 315, 303, 300,
+    299, 312, 301, 283, 290, 285, 321, 331, 288, 320, 289, 319, 324, 287, 286, 322, 323, 327, 304, 284, 306,
+    293, 291, 337, 292, 338, 339, 341, 297, 340, 307, 342, 296, 325, 328, 326, 330, 311, 310, 308, 362, 366,
+    364, 365, 294, 363, 344, 295, 329, 345, 351, 332, 333, 336, 334, 335, 355, 309, 343, 346, 347, 386, 389,
+    367, 388, 371, 372, 390, 369, 379, 387, 368, 375, 370, 374, 378, 373, 376, 349, 352, 348, 391, 396, 395,
+    393, 403, 392, 399, 350, 354, 394, 398, 397, 400, 402, 377, 380, 353, 381, 384, 382, 385, 383, 356, 357,
+    358, 361, 360, 359, 401, 404, 405, 408, 407, 406, 409,
 )
 MESSAGES = 331
 

time: 174 us -> 175 us (level)
  no operation moved by 1% of the time
where the time goes in v6:
time: 175 us
  Pallas kernels  174 us (99%)
    pallas_call x1, Pallas kernels, per_device(): pl.pallas_call(kernel, name='cross_attention', out_shape=shapes, in_specs...  172 us

profile of v6, /device:TPU:0, one launch (start us, length us, event | category | flops | bytes accessed | tf_op | source)
XLA Modules:
  0.0 174.5 jit_solution(4340614079443497414)
XLA Ops:
  0.6 171.7 %cross_attention.1 = (bf16[512,256]{1,0:T(8,128)(2,1)}, bf16[512,256]{1,0:T(8,128)(2,1)}, bf16[8,128,256]{2,1,0:T(8,128)(2,1)}) custom-call(bf16[1024,256]{1,0:T(8,128)(2,1)} %bitcast.2, bf16[512,256]{1,0:T(8,128)(2,1)} %refs_1_.1, bf16[512,256]{1,0:T(8,128)(2,1)} %refs_2_.1, bf16[4096,256]{1,0:T(8,128)(2,1)} %refs_3_.1, bf16[4096,256]{1,0:T(8,128)(2,1)} %refs_4_.1, ...), custom_call_target="tpu_custom_call" | custom-call | tf_op jit(solution)/shard_map/cross_attention/pallas_call | solution.py:715
  172.3 2.2 %hand_over.1 = (bf16[512,256]{1,0:T(8,128)(2,1)}, bf16[512,256]{1,0:T(8,128)(2,1)}, bf16[8,128,256]{2,1,0:T(8,128)(2,1)}) custom-call(bf16[512,256]{1,0:T(8,128)(2,1)} %get-tuple-element.6.refs_0_, bf16[512,256]{1,0:T(8,128)(2,1)} %get-tuple-element.7.refs_1_, bf16[8,128,256]{2,1,0:T(8,128)(2,1)} %get-tuple-element.8.refs_2_), custom_call_target="tpu_custom_call" | custom-call | tf_op jit(solution)/shard_map/hand_over/pallas_call | solution.py:728

commit v7 on v6

--- a/solution.py
+++ b/solution.py
@@ -34,29 +34,29 @@
 OFFSETS = (0, 3, 1, 2)
 SHARES = {"K": (256, 256), "V": (256,), "Q": (256,), "O": ()}
 ALONE = 256
-UNROLL = 2
+UNROLL = 4
 
 
 ORDER = (
-    0, 35, 81, 127, 184, 200, 216, 219, 99, 18, 106, 218, 1, 164, 107, 2, 280, 187, 19, 82, 171, 4, 7, 8, 20,
-    22, 23, 113, 3, 110, 108, 60, 103, 5, 6, 185, 168, 109, 166, 100, 111, 227, 21, 54, 120, 186, 195, 175,
-    188, 53, 86, 12, 112, 115, 28, 117, 87, 202, 11, 25, 37, 62, 64, 74, 190, 124, 102, 104, 191, 56, 199,
-    201, 55, 196, 67, 75, 57, 58, 16, 92, 27, 39, 114, 205, 9, 32, 10, 61, 24, 29, 192, 36, 101, 206, 59, 78,
-    15, 197, 69, 163, 76, 189, 31, 26, 96, 207, 77, 68, 194, 116, 226, 63, 79, 118, 13, 198, 65, 14, 43, 42,
-    220, 204, 33, 208, 38, 41, 224, 83, 165, 30, 40, 193, 213, 173, 209, 80, 167, 119, 225, 122, 142, 17, 70,
-    221, 228, 47, 84, 212, 170, 169, 34, 214, 157, 45, 44, 230, 231, 46, 89, 85, 88, 235, 236, 66, 237, 232,
-    73, 121, 72, 238, 51, 247, 144, 217, 91, 150, 159, 149, 233, 172, 234, 174, 161, 250, 251, 49, 146, 48,
-    93, 105, 71, 90, 50, 123, 129, 128, 222, 223, 239, 241, 95, 243, 176, 125, 52, 248, 249, 203, 143, 151,
-    229, 156, 94, 154, 97, 246, 252, 253, 245, 130, 131, 152, 133, 132, 153, 136, 271, 211, 210, 135, 244,
-    240, 126, 98, 242, 145, 177, 254, 215, 158, 256, 134, 147, 160, 260, 178, 261, 155, 255, 265, 263, 267,
-    264, 137, 268, 139, 259, 148, 138, 140, 262, 257, 266, 162, 179, 181, 180, 182, 272, 258, 274, 275, 273,
-    141, 269, 183, 276, 277, 270, 281, 278, 282, 313, 279, 298, 302, 305, 314, 316, 318, 317, 315, 303, 300,
-    299, 312, 301, 283, 290, 285, 321, 331, 288, 320, 289, 319, 324, 287, 286, 322, 323, 327, 304, 284, 306,
-    293, 291, 337, 292, 338, 339, 341, 297, 340, 307, 342, 296, 325, 328, 326, 330, 311, 310, 308, 362, 366,
-    364, 365, 294, 363, 344, 295, 329, 345, 351, 332, 333, 336, 334, 335, 355, 309, 343, 346, 347, 386, 389,
-    367, 388, 371, 372, 390, 369, 379, 387, 368, 375, 370, 374, 378, 373, 376, 349, 352, 348, 391, 396, 395,
-    393, 403, 392, 399, 350, 354, 394, 398, 397, 400, 402, 377, 380, 353, 381, 384, 382, 385, 383, 356, 357,
-    358, 361, 360, 359, 401, 404, 405, 408, 407, 406, 409,
+    0, 35, 81, 127, 184, 200, 216, 188, 219, 187, 106, 2, 19, 67, 218, 18, 280, 114, 189, 202, 217, 196, 74,
+    110, 108, 113, 75, 69, 21, 8, 22, 4, 25, 195, 208, 71, 1, 116, 100, 186, 24, 118, 23, 7, 194, 82, 76, 60,
+    107, 37, 28, 78, 115, 117, 77, 79, 12, 199, 185, 29, 102, 54, 104, 6, 5, 53, 192, 80, 119, 99, 68, 32, 86,
+    163, 109, 39, 42, 150, 20, 11, 164, 64, 111, 87, 16, 3, 36, 56, 205, 43, 191, 112, 58, 33, 61, 55, 27,
+    214, 198, 92, 70, 190, 103, 72, 165, 57, 10, 62, 209, 152, 9, 221, 26, 15, 166, 193, 47, 224, 197, 222,
+    38, 59, 168, 204, 154, 220, 120, 223, 84, 40, 31, 96, 63, 149, 225, 227, 83, 14, 41, 229, 73, 169, 65,
+    230, 13, 30, 135, 167, 226, 121, 51, 44, 45, 212, 228, 232, 235, 236, 233, 234, 124, 151, 17, 85, 247,
+    122, 46, 203, 89, 137, 250, 123, 101, 49, 34, 129, 251, 231, 48, 88, 128, 157, 91, 237, 238, 125, 271, 50,
+    90, 136, 93, 210, 201, 177, 211, 105, 126, 248, 95, 52, 249, 239, 246, 242, 215, 131, 94, 130, 159, 142,
+    241, 245, 171, 240, 66, 97, 207, 206, 138, 252, 253, 161, 140, 133, 179, 170, 243, 213, 143, 98, 244, 144,
+    156, 178, 141, 134, 146, 254, 258, 173, 267, 260, 255, 263, 175, 262, 265, 139, 257, 132, 155, 266, 145,
+    264, 261, 172, 147, 174, 158, 268, 256, 160, 180, 182, 181, 153, 274, 275, 259, 148, 272, 273, 176, 162,
+    269, 183, 276, 277, 270, 282, 278, 281, 313, 279, 298, 302, 301, 305, 314, 318, 317, 316, 303, 300, 304,
+    299, 315, 283, 286, 290, 321, 287, 320, 285, 327, 319, 324, 323, 288, 293, 289, 284, 297, 306, 337, 291,
+    322, 331, 338, 340, 342, 339, 296, 341, 307, 311, 292, 325, 328, 308, 326, 330, 312, 362, 366, 364, 363,
+    295, 309, 365, 345, 329, 294, 355, 310, 346, 343, 332, 333, 334, 336, 335, 348, 344, 347, 386, 388, 387,
+    367, 372, 390, 371, 368, 375, 389, 369, 379, 370, 373, 376, 374, 378, 350, 351, 354, 349, 352, 391, 396,
+    395, 392, 399, 393, 403, 394, 397, 398, 400, 402, 377, 380, 381, 385, 382, 383, 384, 353, 356, 357, 358,
+    360, 361, 359, 404, 401, 405, 409, 408, 407, 406,
 )
 MESSAGES = 331
 

time: 175 us -> 171 us (0.977)
  Pallas kernels: 174 us -> 170 us
    pallas_call x1, Pallas kernels: 172 us -> 168 us  [per_device(): pl.pallas_call(kernel, name='cross_attention', out_shape=shapes, in_specs...]
where the time goes in v7:
time: 171 us
  Pallas kernels  170 us (99%)
    pallas_call x1, Pallas kernels, per_device(): pl.pallas_call(kernel, name='cross_attention', out_shape=shapes, in_specs...  168 us

profile of v7, /device:TPU:0, one launch (start us, length us, event | category | flops | bytes accessed | tf_op | source)
XLA Modules:
  0.0 170.7 jit_solution(11716167211306681783)
XLA Ops:
  0.6 167.9 %cross_attention.1 = (bf16[512,256]{1,0:T(8,128)(2,1)}, bf16[512,256]{1,0:T(8,128)(2,1)}, bf16[8,128,256]{2,1,0:T(8,128)(2,1)}) custom-call(bf16[1024,256]{1,0:T(8,128)(2,1)} %bitcast.2, bf16[512,256]{1,0:T(8,128)(2,1)} %refs_1_.1, bf16[512,256]{1,0:T(8,128)(2,1)} %refs_2_.1, bf16[4096,256]{1,0:T(8,128)(2,1)} %refs_3_.1, bf16[4096,256]{1,0:T(8,128)(2,1)} %refs_4_.1, ...), custom_call_target="tpu_custom_call" | custom-call | tf_op jit(solution)/shard_map/cross_attention/pallas_call | solution.py:715
  168.5 2.2 %hand_over.1 = (bf16[512,256]{1,0:T(8,128)(2,1)}, bf16[512,256]{1,0:T(8,128)(2,1)}, bf16[8,128,256]{2,1,0:T(8,128)(2,1)}) custom-call(bf16[512,256]{1,0:T(8,128)(2,1)} %get-tuple-element.6.refs_0_, bf16[512,256]{1,0:T(8,128)(2,1)} %get-tuple-element.7.refs_1_, bf16[8,128,256]{2,1,0:T(8,128)(2,1)} %get-tuple-element.8.refs_2_), custom_call_target="tpu_custom_call" | custom-call | tf_op jit(solution)/shard_map/hand_over/pallas_call | solution.py:728
